TPU v7x, 32 devices: a whole 2x2x4 slice. The times are simulated.
32 devices in a mesh: img: 8 (over z, x), band: 4 (over y, core).
Axes of the slice: x: 2, y: 2, z: 4, core: 2. Of those that a mesh axis runs over, the one named last changes fastest.
Arguments:
- images: bfloat16 [32, 32, 32, 512], P('img', 'band'), may hold values from -18 to 18
- cotangent: bfloat16 [32, 32, 32, 512], P('img', 'band'), may hold values from -6 to 6
- sizes: int32 [32], P('img'), may hold values from 16 to 32, as said below
- matrix_weight: float32 [5767168], P(('img', 'band')), may hold values from -0.8838835 to 0.8838835
- matrix_momentum: float32 [5767168], P(('img', 'band')), may hold values from -512 to 512
- matrix_average: float32 [5767168], P(('img', 'band')), may hold values from -0.8838835 to 0.8838835
- vector_weight: float32 [11, 512], replicated, may hold values from -0.3 to 1.45
- vector_momentum: float32 [11, 512], replicated, may hold values from -512 to 512
- vector_average: float32 [11, 512], replicated, may hold values from -0.3 to 1.45
Outputs:
- block_out: bfloat16 [32, 32, 32, 512], P('img', 'band')
- input_grad: float32 [32, 32, 32, 512], P('img', 'band')
- matrix_grads: float32 [5767168], P(('img', 'band'))
- matrix_moments: float32 [5767168], P(('img', 'band'))
- matrix_means: float32 [5767168], P(('img', 'band'))
- matrix_masters: float32 [5767168], P(('img', 'band'))
- vector_grads: float32 [11, 512], replicated
- vector_moments: float32 [11, 512], replicated
- vector_means: float32 [11, 512], replicated
- vector_masters: float32 [11, 512], replicated
Inputs may be any that keep to these rules, and one draw needn't show every extreme that they name: `sizes`: each value is 16, 24 or 32; among images 4 k to 4 k + 3 at least one has size 32.
All inputs are finite; a program needn't handle non-finite values.
Results may differ from a plain program's by a relative error of at most 0.013.
The roundings to bfloat16 on the way count: a program that leaves them out, or rounds other values in their place, can miss the bound.
Values may be sent and summed in bfloat16 or wider, within the bound.
No kernel may reach another device: no remote copies, remote signals or barrier semaphores. Data moves between devices by JAX's collectives and lax.ppermute only.
A program may use at most 192 MiB of HBM per device.

v0:
```python
import jax
import jax.numpy as jnp
from jax import lax
from jax.sharding import PartitionSpec as P

GROUPS = 32


EPS = 1e-06
MOMENTUM = 0.9
LR_MATRIX = 4e-05
LR_VECTOR = 0.0001
AVERAGE = 0.75


def extended(array, sides, width):
    for axis, dim in sides:
        count, length = (lax.axis_size(axis), array.shape[dim])
        up = [(i, (i + 1) % count) for i in range(count - 1)]
        down = [(j, i) for i, j in up]
        last = lax.slice_in_dim(array, length - width, length, axis=dim)
        initial = lax.slice_in_dim(array, 0, width, axis=dim)
        before = lax.ppermute(last, axis, up)
        after = lax.ppermute(initial, axis, down)
        array = jnp.concatenate([before, array, after], axis=dim)
    return array


def split_groups(field):
    return field.reshape(field.shape[:3] + (GROUPS, field.shape[3] // GROUPS))


def group_sums(field, mask):
    shaped = split_groups(field)
    weighted = shaped * mask[..., None]
    return (jnp.sum(weighted, axis=(1, 2, 4)), jnp.sum(weighted * shaped, axis=(1, 2, 4)))


def group_apply(field, sums, count, gain, shift):
    center = sums[0] / count[:, None]
    spread = sums[1] / count[:, None] - center * center
    scale = lax.rsqrt(spread + EPS)
    shaped = split_groups(field)
    normed = (shaped - center[:, None, None, :, None]) * scale[:, None, None, :, None]
    return normed.reshape(field.shape) * gain + shift


def normalize(field, mask, count, gain, shift):
    sums = lax.psum(group_sums(field, mask), "band")
    return (group_apply(field, sums, count, gain, shift), sums)


def normalize_back(field, sums, mask, count, gain, shift, upstream):
    _, pull = jax.vjp(
        lambda field_in, sums_in, gain_in, shift_in: group_apply(
            field_in, sums_in, count, gain_in, shift_in
        ),
        field,
        sums,
        gain,
        shift,
    )
    direct, grad_sums, grad_gain, grad_shift = pull(upstream)
    grad_sums = lax.psum(grad_sums, "band")
    _, pull_sums = jax.vjp(lambda field_in: group_sums(field_in, mask), field)
    return (direct + pull_sums(grad_sums)[0], grad_gain, grad_shift)


def activate(field, mask):
    return jax.nn.silu(field) * mask


def activate_back(field, mask, upstream):
    _, pull = jax.vjp(lambda inner: activate(inner, mask), field)
    return pull(upstream)[0]


def widen(field):
    return jnp.pad(field, ((0, 0), (0, 0), (1, 1), (0, 0)))


def taps(padded, kernel, height, width):
    total = jnp.zeros(padded.shape[:1] + (height, width, kernel.shape[2]), jnp.float32)
    for tap in range(9):
        row, column = (tap // 3, tap % 3)
        total = total + jnp.einsum(
            "ghwc,cd->ghwd",
            padded[:, row : row + height, column : column + width],
            kernel[tap],
            preferred_element_type=jnp.float32,
        )
    return total


def conv_forward(low_field, kernel):
    padded = widen(extended(low_field, (("band", 1),), 1))
    return (taps(padded, kernel, low_field.shape[1], low_field.shape[2]), padded)


def conv_backward(low_grad, kernel, padded):
    height, width = (low_grad.shape[1], low_grad.shape[2])
    grad_pad = widen(extended(low_grad, (("band", 1),), 1))
    flipped = jnp.swapaxes(kernel[::-1], 1, 2)
    grad_in = taps(grad_pad, flipped, height, width)
    pieces = []
    for tap in range(9):
        row, column = (tap // 3, tap % 3)
        pieces.append(
            jnp.einsum(
                "ghwc,ghwd->cd",
                padded[:, row : row + height, column : column + width],
                low_grad,
                preferred_element_type=jnp.float32,
            )
        )
    return (grad_in, jnp.stack(pieces))


def attend(query_low, key_full, key_valid, factor):
    score_matrix = (
        jnp.einsum("gqc,gkc->gqk", query_low, key_full, preferred_element_type=jnp.float32) * factor
    )
    score_matrix = jnp.where(key_valid[:, None, :], score_matrix, -1e30)
    top = jnp.max(score_matrix, axis=2, keepdims=True)
    raised = jnp.exp(score_matrix - top)
    total = jnp.sum(raised, axis=2, keepdims=True)
    return (raised / total, top, total)


def per_device(
    images,
    cotangent,
    sizes,
    matrix_weight,
    matrix_momentum,
    matrix_average,
    vector_weight,
    vector_momentum,
    vector_average,
):
    batch, height, width, channels = images.shape
    square = channels * channels
    queries = height * width
    positions = width * width
    factor = channels ** (-0.5)
    weights = lax.all_gather(
        matrix_weight.astype(jnp.bfloat16), ("img", "band"), axis=0, tiled=True
    )
    kernel_one = weights[: 9 * square].reshape(9, channels, channels)
    kernel_two = weights[9 * square : 18 * square].reshape(9, channels, channels)
    attn_in = weights[18 * square : 21 * square].reshape(3, channels, channels)
    attention_output = weights[21 * square :].reshape(channels, channels)
    lines = lax.axis_index("band") * height + jnp.arange(height)
    across = jnp.arange(width)
    limit = sizes[:, None, None]
    inside = (lines[None, :, None] < limit) & (across[None, None, :] < limit)
    mask = jnp.where(inside, 1.0, 0.0).astype(jnp.float32)[..., None]
    count = (sizes * sizes * (channels // GROUPS)).astype(jnp.float32)
    spots = jnp.arange(positions)
    key_valid = ((spots // width)[None, :] < sizes[:, None]) & (
        (spots % width)[None, :] < sizes[:, None]
    )
    start = images.astype(jnp.float32) * mask
    norm_one, sums_one = normalize(start, mask, count, vector_weight[0], vector_weight[1])
    act_one = activate(norm_one, mask).astype(jnp.bfloat16)
    conv_raw, padded_one = conv_forward(act_one, kernel_one)
    conv_out = conv_raw + vector_weight[2]
    norm_two, sums_two = normalize(conv_out, mask, count, vector_weight[3], vector_weight[4])
    act_two = activate(norm_two, mask).astype(jnp.bfloat16)
    conv_raw, padded_two = conv_forward(act_two, kernel_two)
    resid = (start + conv_raw + vector_weight[5]) * mask
    norm_three, sums_three = normalize(resid, mask, count, vector_weight[6], vector_weight[7])
    normed = (norm_three * mask).astype(jnp.bfloat16).reshape(batch, queries, channels)
    projected = jnp.einsum("gqc,jcd->jgqd", normed, attn_in, preferred_element_type=jnp.float32)
    query_low = (projected[0] + vector_weight[8]).astype(jnp.bfloat16)
    key_low = projected[1].astype(jnp.bfloat16)
    value_low = (projected[2] + vector_weight[9]).astype(jnp.bfloat16)
    key_full, value_full = (
        lax.all_gather(key_low, "band", axis=1, tiled=True),
        lax.all_gather(value_low, "band", axis=1, tiled=True),
    )
    probability_rows, row_top, row_total = attend(query_low, key_full, key_valid, factor)
    mixed_values = jnp.einsum(
        "gqk,gkc->gqc",
        probability_rows.astype(jnp.bfloat16),
        value_full,
        preferred_element_type=jnp.float32,
    ).astype(jnp.bfloat16)
    output_rows = (
        jnp.einsum(
            "gqc,cd->gqd", mixed_values, attention_output, preferred_element_type=jnp.float32
        )
        + vector_weight[10]
    )
    block_out = ((resid + output_rows.reshape(images.shape)) * mask).astype(jnp.bfloat16)
    grad_top = cotangent.astype(jnp.float32) * mask
    grad_proj = grad_top.reshape(batch, queries, channels)
    grad_proj_low = grad_proj.astype(jnp.bfloat16)
    grad_out_weight = jnp.einsum(
        "gqc,gqd->cd", mixed_values, grad_proj_low, preferred_element_type=jnp.float32
    )
    grad_mixed = jnp.einsum(
        "gqd,cd->gqc", grad_proj_low, attention_output, preferred_element_type=jnp.float32
    ).astype(jnp.bfloat16)
    back_keys, back_values = (
        lax.all_gather(key_low, "band", axis=1, tiled=True),
        lax.all_gather(value_low, "band", axis=1, tiled=True),
    )
    back_probs = attend(query_low, back_keys, key_valid, factor)[0]
    grad_probs = jnp.einsum(
        "gqc,gkc->gqk", grad_mixed, back_values, preferred_element_type=jnp.float32
    )
    weighted_sum = jnp.sum(back_probs * grad_probs, axis=2, keepdims=True)
    grad_scores = back_probs * (grad_probs - weighted_sum)
    grad_scores_low = (grad_scores * factor).astype(jnp.bfloat16)
    grad_query = jnp.einsum(
        "gqk,gkc->gqc", grad_scores_low, back_keys, preferred_element_type=jnp.float32
    ).astype(jnp.bfloat16)
    key_terms = jnp.einsum(
        "gqk,gqc->gkc", grad_scores_low, query_low, preferred_element_type=jnp.float32
    )
    value_terms = jnp.einsum(
        "gqk,gqc->gkc",
        back_probs.astype(jnp.bfloat16),
        grad_mixed,
        preferred_element_type=jnp.float32,
    )
    grad_key, grad_value = (
        lax.psum_scatter(
            key_terms.astype(jnp.bfloat16), "band", scatter_dimension=1, tiled=True
        ).astype(jnp.float32),
        lax.psum_scatter(
            value_terms.astype(jnp.bfloat16), "band", scatter_dimension=1, tiled=True
        ).astype(jnp.float32),
    )
    grad_value_low = grad_value.astype(jnp.bfloat16)
    grads_low = jnp.stack([grad_query, grad_key.astype(jnp.bfloat16), grad_value_low])
    grad_in_weights = jnp.einsum(
        "gqc,jgqd->jcd", normed, grads_low, preferred_element_type=jnp.float32
    )
    grad_normed = (
        jnp.einsum("jgqd,jcd->gqc", grads_low, attn_in, preferred_element_type=jnp.float32).reshape(
            images.shape
        )
        * mask
    )
    grad_resid_norm, grad_gain_three, grad_shift_three = normalize_back(
        resid, sums_three, mask, count, vector_weight[6], vector_weight[7], grad_normed
    )
    grad_resid = (grad_top + grad_resid_norm) * mask
    grad_act_two, grad_kernel_two = conv_backward(
        grad_resid.astype(jnp.bfloat16), kernel_two, padded_two
    )
    grad_norm_two = activate_back(norm_two, mask, grad_act_two)
    grad_conv_out, grad_gain_two, grad_shift_two = normalize_back(
        conv_out, sums_two, mask, count, vector_weight[3], vector_weight[4], grad_norm_two
    )
    grad_act_one, grad_kernel_one = conv_backward(
        grad_conv_out.astype(jnp.bfloat16), kernel_one, padded_one
    )
    grad_norm_one = activate_back(norm_one, mask, grad_act_one)
    grad_start, grad_gain_one, grad_shift_one = normalize_back(
        start, sums_one, mask, count, vector_weight[0], vector_weight[1], grad_norm_one
    )
    input_grad = (grad_resid + grad_start) * mask
    vector_terms = jnp.stack(
        [
            grad_gain_one,
            grad_shift_one,
            jnp.sum(grad_conv_out, axis=(0, 1, 2)),
            grad_gain_two,
            grad_shift_two,
            jnp.sum(grad_resid, axis=(0, 1, 2)),
            grad_gain_three,
            grad_shift_three,
            jnp.sum(grad_query, axis=(0, 1), dtype=jnp.float32),
            jnp.sum(grad_value_low, axis=(0, 1), dtype=jnp.float32),
            jnp.sum(grad_proj, axis=(0, 1)),
        ]
    )
    vector_grads = lax.psum(vector_terms, ("img", "band"))
    grad_flat = jnp.concatenate(
        [
            grad_kernel_one.reshape(-1),
            grad_kernel_two.reshape(-1),
            grad_in_weights.reshape(-1),
            grad_out_weight.reshape(-1),
        ]
    )
    matrix_grads = lax.psum_scatter(grad_flat, ("img", "band"), scatter_dimension=0, tiled=True)
    matrix_moments = MOMENTUM * matrix_momentum + matrix_grads
    matrix_masters = matrix_weight - LR_MATRIX * (matrix_grads + MOMENTUM * matrix_moments)
    matrix_means = AVERAGE * matrix_average + (1.0 - AVERAGE) * matrix_masters
    vector_moments = MOMENTUM * vector_momentum + vector_grads
    vector_masters = vector_weight - LR_VECTOR * (vector_grads + MOMENTUM * vector_moments)
    vector_means = AVERAGE * vector_average + (1.0 - AVERAGE) * vector_masters
    return (
        block_out,
        input_grad,
        matrix_grads,
        matrix_moments,
        matrix_means,
        matrix_masters,
        vector_grads,
        vector_moments,
        vector_means,
        vector_masters,
    )


def solution(mesh):
    return jax.shard_map(
        per_device,
        mesh=mesh,
        in_specs=(
            P("img", "band", None, None),
            P("img", "band", None, None),
            P("img"),
            P(("img", "band")),
            P(("img", "band")),
            P(("img", "band")),
            P(),
            P(),
            P(),
        ),
        out_specs=(
            P("img", "band", None, None),
            P("img", "band", None, None),
            P(("img", "band")),
            P(("img", "band")),
            P(("img", "band")),
            P(("img", "band")),
            P(),
            P(),
            P(),
            P(),
        ),
        check_vma=False,
    )
```

profile of v0, /device:TPU:0, one launch (start us, length us, event | category | flops | bytes accessed | tf_op | source)
XLA Modules:
  0.0 883.1 jit_solution(6961672429460320519)
XLA Ops:
  11.8 8.4 all-reduce.10
  26.1 2.5 collective-permute-done.1
  29.5 75.9 %all-gather.5.cloned.1.call-done = bf16[5767168]{0:T(1024)(128)(2,1)} async-done(((bf16[180224]{0:T(1024)(128)(2,1)}), bf16[5767168]{0:T(1024)(128)(2,1)}) %all-gather.5.cloned.1.call-update) | async-done | bytes 11534352 | tf_op jit(solution)/shard_map/all_gather | solution.py:146
  105.4 7.4 fusion.234
  112.8 2.2 reshape.569
  114.9 2.1 reshape.564
  117.1 2.1 reshape.563
  119.2 2.1 reshape.562
  121.4 2.2 reshape.561
  123.6 2.2 reshape.560
  125.7 2.1 reshape.559
  127.9 2.2 reshape.558
  130.1 2.2 reshape.557
  132.2 2.2 reshape.556
  143.8 2.5 multiply_reduce_fusion.2
  146.7 7.2 all-reduce.9
  155.0 2.4 multiply_convert_fusion.3
  160.8 2.2 fusion.174
  162.9 2.7 slice.770
  165.6 3.8 reshape.575
  169.4 2.2 reshape.573
  173.8 2.2 reshape.570
  178.2 2.2 reshape.567
  193.9 8.0 all-reduce.8
  205.6 2.6 copy-done.20
  209.5 2.9 fusion.31
  213.7 2.2 convolution_convert_fusion.3
  215.9 27.7 %all-gather.9.cloned.1.call-done = bf16[1,4,1024,512]{3,2,0,1:T(8,128)(2,1)} async-done(((bf16[1,4,256,512]{3,2,0,1:T(8,128)(2,1)}), bf16[1,4,1024,512]{3,2,0,1:T(8,128)(2,1)}) %all-gather.9.cloned.1.call-update) | async-done | bytes 4194320 | tf_op jit(solution)/shard_map/all_gather | solution.py:179
  243.6 4.1 fusion.4
  251.6 3.6 convolution_convert_fusion
  255.2 24.5 %all-gather.7.cloned.1.call-done = bf16[4,1024,512]{2,1,0:T(8,128)(2,1)} async-done(((bf16[4,256,512]{2,1,0:T(8,128)(2,1)}), bf16[4,1024,512]{2,1,0:T(8,128)(2,1)}) %all-gather.7.cloned.1.call-update) | async-done | bytes 4194320 | tf_op jit(solution)/shard_map/all_gather | solution.py:180
  279.7 5.4 fusion.243
  285.1 17.1 %convolution_convert_fusion.1 = bf16[4,1024,512]{2,1,0:T(8,128)(2,1)} fusion(f32[4,256,1024]{2,1,0:T(8,128)} %fusion.243, f32[3,4,256,512]{3,2,0,1:T(8,128)} %copy-done.20, f32[512]{0:T(512)S(1)} %bitcast.496, f32[4,256,1024]{2,1,0:T(8,128)} %copy-done.98, f32[4,256]{1,0:T(4,128)S(1)} %get-tuple-element.116), kind=kOutput, calls=%fused_computation.33 | convolution fusion | flops 1084229632 | bytes 23078912 | tf_op jit(solution)/shard_map/gqk,gqc->gkc/dot_general | solution.py:219
  302.5 8.3 fusion.233
  310.8 3.7 reshape.577
  314.5 8.5 slice.698
  323.0 6.7 copy.36
  329.7 5.3 reverse_bitcast_fusion.1
  341.9 13.5 %convert_reduce_fusion.1 = (f32[512]{0:T(512)}, bf16[4,256,512]{2,1,0:T(8,128)(2,1)S(1)}) fusion(bf16[1,4,1024,512]{3,2,0,1:T(8,128)(2,1)} %all-gather.9.cloned.1.call-done, f32[4,256,1024]{2,1,0:T(8,128)} %fusion.243, f32[4,256,1024]{2,1,0:T(8,128)} %copy-done.98, f32[4,256]{1,0:T(4,128)S(1)} %get-tuple-element.116), kind=kOutput, calls=%fused_computation.61 | convolution fusion | flops 1082656256 | bytes 13637632 | tf_op jit(solution)/shard_map/gqk,gkc->gqc/dot_general | solution.py:216
  355.4 18.3 %reduce-scatter.3.cloned.1.call-done = bf16[4,256,512]{2,1,0:T(8,128)(2,1)} async-done(((bf16[4,1024,512]{2,1,0:T(8,128)(2,1)}), bf16[4,256,512]{2,1,0:T(8,128)(2,1)}) %reduce-scatter.3.cloned.1.call-update) | async-done | bytes 1048592 | tf_op jit(solution)/shard_map/reduce_scatter | solution.py:229
  379.7 5.7 all-reduce.7
  385.8 4.3 fusion.225
  394.5 3.5 convolution_bitcast_fusion.1
  407.3 3.6 copy-done.16
  411.0 3.1 fusion.169
  414.0 3.5 copy.39
  417.6 4.3 copy.104
  421.9 9.7 %copy.103 = f32[576,4,8,128]{3,1,2,0:T(4,128)} copy(f32[576,4,8,128]{3,2,1,0:T(8,128)} %bitcast.460) | data formatting | bytes 18874368
  442.6 3.8 multiply_reduce_fusion.8
  446.8 8.4 all-reduce.6
  455.6 2.4 fusion.224
  465.5 3.6 copy-done.17
  469.1 9.7 %copy.102 = f32[576,4,8,128]{3,1,2,0:T(4,128)} copy(f32[576,4,8,128]{3,2,1,0:T(8,128)} %bitcast.461) | data formatting | bytes 18874368
  478.8 24.9 %pad_maximum_fusion = f32[5767168]{0:T(1024)} fusion(f32[262144]{0:T(1024)S(1)} %bitcast.462, f32[786432]{0:T(1024)} %bitcast.456, f32[2359296]{0:T(1024)} %bitcast.454, f32[2359296]{0:T(1024)} %bitcast.455), kind=kLoop, calls=%fused_computation.2 | loop fusion | flops 17301504 | bytes 46137344 | tf_op jit(solution)/shard_map/concatenate | solution.py:282
  503.8 8.6 slice.719
  512.5 6.9 copy.37
  519.4 2.8 reverse_bitcast_fusion
  526.2 2.7 collective-permute-done.7
  540.0 7.3 multiply_reduce_fusion.5
  547.8 11.6 %all-reduce.5 = (f32[4,32]{1,0:T(4,128)S(1)}, f32[4,32]{1,0:T(4,128)S(1)}) all-reduce(f32[4,32]{1,0:T(4,128)S(1)} %get-tuple-element.106, f32[4,32]{1,0:T(4,128)S(1)} %get-tuple-element.105), channel_id=1, replica_groups=mesh['img'=8,'band'=4] {'band'}, use_global_device_ids=true, to_apply=%region_40.41 | all-reduce | flops 256 | bytes 2048 | tf_op jit(solution)/shard_map/psum | solution.py:64
  559.9 42.1 %psum.103 = f32[11,512]{1,0:T(8,128)S(1)} all-reduce(f32[11,512]{1,0:T(8,128)S(1)} %stack.143), channel_id=1, replica_groups=mesh['img'=8,'band'=4] {'img','band'}, use_global_device_ids=true, to_apply=%region_53.54 | all-reduce | flops 5632 | bytes 45056 | tf_op jit(solution)/shard_map/psum | solution.py:281
  602.7 4.0 fusion.17
  606.7 265.8 %all-reduce.13.cloned.1.call-done = f32[5767168]{0:T(1024)} async-done(((f32[5767168]{0:T(1024)}), f32[5767168]{0:T(1024)}) %all-reduce.13.cloned.1.call-update) | async-done | bytes 23068688
  872.5 3.5 multiply_add_fusion.2
  (372 shorter events, 115.7 us)
Async XLA Ops:
  7.2 13.0 %copy-start.97 = (s32[4]{0:T(128)S(1)}, s32[4]{0:T(128)}, u32[]{:S(2)}) copy-start(s32[4]{0:T(128)} %param.11) | copy-start | bytes 52
  7.2 3.7 copy-start.8
  7.2 14.0 %copy-start.67 = (f32[11,512]{1,0:T(8,128)S(1)}, f32[11,512]{1,0:T(8,128)}, u32[]{:S(2)}) copy-start(f32[11,512]{1,0:T(8,128)} %param.15) | copy-start | bytes 67588
  7.2 14.1 %copy-start.25 = (bf16[4,8,32,512]{3,2,1,0:T(8,128)(2,1)S(1)}, bf16[4,8,32,512]{3,2,1,0:T(8,128)(2,1)}, u32[]{:S(2)}) copy-start(bf16[4,8,32,512]{3,2,1,0:T(8,128)(2,1)} %param.10) | copy-start | bytes 3145732
  7.2 98.2 %all-gather.5.cloned.1.call-start = ((), (), s32[]{:S(2)}) async-start(), calls=%async_computation.2 | async-start | bytes 11894784 | tf_op jit(solution)/shard_map/all_gather | solution.py:146
  9.3 234.3 %all-gather.9.cloned.1.call-start = ((), (), s32[]{:S(2)}) async-start(), calls=%async_computation.6 | async-start | bytes 5242880 | tf_op jit(solution)/shard_map/all_gather | solution.py:179
  21.3 133.7 %copy-start.81 = (f32[1,512]{1,0:T(1,128)}, f32[1,512]{1,0:T(1,128)S(1)}, u32[]{:S(2)}) copy-start(f32[1,512]{1,0:T(1,128)S(1)} %get-tuple-element.99) | copy-start | bytes 6148
  21.3 133.7 %copy-start.87 = (f32[1,512]{1,0:T(1,128)}, f32[1,512]{1,0:T(1,128)S(1)}, u32[]{:S(2)}) copy-start(f32[1,512]{1,0:T(1,128)S(1)} %get-tuple-element.98) | copy-start | bytes 6148
  23.4 5.2 copy-start.10
  23.5 2.6 collective-permute-start
  24.8 3.8 collective-permute-start.1
  26.1 115.3 %copy-start.62 = (bf16[4,1,32,512]{3,2,1,0:T(8,128)(2,1)}, bf16[4,1,32,512]{3,2,1,0:T(8,128)(2,1)S(1)}, u32[]{:S(2)}) copy-start(bf16[4,1,32,512]{3,2,1,0:T(8,128)(2,1)S(1)} %collective-permute-done) | copy-start | bytes 393220
  28.6 113.8 %copy-start.60 = (bf16[4,1,32,512]{3,2,1,0:T(8,128)(2,1)}, bf16[4,1,32,512]{3,2,1,0:T(8,128)(2,1)S(1)}, u32[]{:S(2)}) copy-start(bf16[4,1,32,512]{3,2,1,0:T(8,128)(2,1)S(1)} %collective-permute-done.1) | copy-start | bytes 393220
  29.5 114.0 %copy-start.2 = (bf16[4,10,34,512]{3,2,1,0:T(8,128)(2,1)}, bf16[4,10,34,512]{3,2,1,0:T(8,128)(2,1)S(1)}, u32[]{:S(2)}) copy-start(bf16[4,10,34,512]{3,2,1,0:T(8,128)(2,1)S(1)} %fusion.49) | copy-start | bytes 4177924
  146.5 14.2 %copy-start.33 = (bf16[512,512,1,1]{1,0,2,3:T(8,128)(2,1)S(1)}, bf16[512,512,1,1]{1,0,2,3:T(8,128)(2,1)}, u32[]{:S(2)}) copy-start(bf16[512,512,1,1]{1,0,2,3:T(8,128)(2,1)} %reshape.569) | copy-start | bytes 1572868
  154.0 9.0 %copy-start.92 = (f32[4,32]{1,0:T(4,128)}, f32[4,32]{1,0:T(4,128)S(1)}, u32[]{:S(2)}) copy-start(f32[4,32]{1,0:T(4,128)S(1)} %get-tuple-element.44) | copy-start | bytes 1540
  154.8 8.1 copy-start.71
  155.0 7.9 copy-start.75
  157.4 32.4 %copy-start.13 = (bf16[4,8,32,512]{3,2,1,0:T(8,128)(2,1)}, bf16[4,8,32,512]{3,2,1,0:T(8,128)(2,1)S(1)}, u32[]{:S(2)}) copy-start(bf16[4,8,32,512]{3,2,1,0:T(8,128)(2,1)S(1)} %multiply_convert_fusion.3) | copy-start | bytes 3145732
  158.2 24.4 %collective-permute-start.2 = (bf16[4,1,32,512]{3,2,1,0:T(8,128)(2,1)}, bf16[4,1,32,512]{3,2,1,0:T(8,128)(2,1)S(1)}, u32[]{:S(2)}, u32[]{:S(2)}) collective-permute-start(bf16[4,1,32,512]{3,2,1,0:T(8,128)(2,1)} %get-tuple-element.88), channel_id=1, source_target_pairs={{0,1},{1,2},{2,3},{4,5},{5,6},{6,7},{8,9},{9,10},{10,11},{12,13},{... | collective-permute-start | bytes 393224 | tf_op jit(solution)/shard_map/ppermute | solution.py:23
  159.5 23.1 %collective-permute-start.3 = (bf16[4,1,32,512]{3,2,1,0:T(8,128)(2,1)}, bf16[4,1,32,512]{3,2,1,0:T(8,128)(2,1)S(1)}, u32[]{:S(2)}, u32[]{:S(2)}) collective-permute-start(bf16[4,1,32,512]{3,2,1,0:T(8,128)(2,1)} %get-tuple-element.89), channel_id=1, source_target_pairs={{1,0},{2,1},{3,2},{5,4},{6,5},{7,6},{9,8},{10,9},{11,10},{13,12},{... | collective-permute-start | bytes 393224 | tf_op jit(solution)/shard_map/ppermute | solution.py:24
  165.6 6.0 copy-start.32
  165.6 7.1 copy-start.31
  172.7 7.6 copy-start.30
  173.8 7.7 copy-start.29
  183.5 7.4 copy-start
  202.8 2.9 copy-start.46
  209.5 70.2 %all-gather.7.cloned.1.call-start = ((), (), s32[]{:S(2)}) async-start(), calls=%async_computation.3 | async-start | bytes 5242880 | tf_op jit(solution)/shard_map/all_gather | solution.py:180
  209.5 3.1 copy-start.28
  212.4 143.0 %reduce-scatter.5.cloned.1.call-start = ((), (), s32[]{:S(2)}) async-start(), calls=%async_computation.5 | async-start | bytes 5242880 | tf_op jit(solution)/shard_map/reduce_scatter | solution.py:232
  255.2 118.6 %reduce-scatter.3.cloned.1.call-start = ((), (), s32[]{:S(2)}) async-start(), calls=%async_computation.4 | async-start | bytes 5242880 | tf_op jit(solution)/shard_map/reduce_scatter | solution.py:229
  302.3 570.2 %all-reduce.13.cloned.1.call-start = ((), (), s32[]{:S(2)}) async-start(), calls=%async_computation.7 | async-start | bytes 46137344
  329.7 5.3 copy-start.22
  329.7 6.7 copy-start.99
  355.4 20.3 %copy-start.49 = (bf16[4,256,512]{2,1,0:T(8,128)(2,1)}, bf16[4,256,512]{2,1,0:T(8,128)(2,1)S(1)}, u32[]{:S(2)}) copy-start(bf16[4,256,512]{2,1,0:T(8,128)(2,1)S(1)} %get-tuple-element.121) | copy-start | bytes 3145732
  377.6 8.2 copy-start.26
  390.1 2.9 copy-start.4
  394.5 6.9 copy-start.14
  397.9 33.7 %collective-permute-start.4 = (bf16[4,1,32,512]{3,2,1,0:T(8,128)(2,1)S(1)}, bf16[4,1,32,512]{3,2,1,0:T(8,128)(2,1)S(1)}, u32[]{:S(2)}, u32[]{:S(2)}) collective-permute-start(bf16[4,1,32,512]{3,2,1,0:T(8,128)(2,1)S(1)} %get-tuple-element.86), channel_id=1, source_target_pairs={{0,1},{1,2},{2,3},{4,5},{5,6},{6,7},{8,9},{9,10},{10,11},{12,13},{... | collective-permute-start | bytes 393224 | tf_op jit(solution)/shard_map/ppermute | solution.py:23
  399.7 32.0 %collective-permute-start.5 = (bf16[4,1,32,512]{3,2,1,0:T(8,128)(2,1)S(1)}, bf16[4,1,32,512]{3,2,1,0:T(8,128)(2,1)S(1)}, u32[]{:S(2)}, u32[]{:S(2)}) collective-permute-start(bf16[4,1,32,512]{3,2,1,0:T(8,128)(2,1)S(1)} %get-tuple-element.87), channel_id=1, source_target_pairs={{1,0},{2,1},{3,2},{5,4},{6,5},{7,6},{9,8},{10,9},{11,10},{13,12},{... | collective-permute-start | bytes 393224 | tf_op jit(solution)/shard_map/ppermute | solution.py:24
  407.3 3.7 copy-start.16
  431.6 2.8 copy-start.64
  432.5 5.5 slice-start
  434.4 3.6 slice-start.1
  442.6 4.2 copy-start.93
  442.6 4.2 copy-start.94
  465.5 3.7 copy-start.17
  469.1 9.7 %copy-start.21 = (f32[64,4,8,128]{3,1,2,0:T(4,128)S(1)}, f32[64,4,8,128]{3,1,2,0:T(4,128)}, u32[]{:S(2)}) copy-start(f32[64,4,8,128]{3,1,2,0:T(4,128)} %copy.105) | copy-start | bytes 3145732
  519.4 2.8 copy-start.24
  522.4 3.8 collective-permute-start.6
  524.2 4.7 collective-permute-start.7
  535.3 3.5 copy-start.27
  536.0 2.8 copy-start.41
  539.9 7.8 copy-start.90
  539.9 7.8 copy-start.91
  539.9 19.9 %copy-start.85 = (f32[512]{0:T(512)S(1)}, f32[512]{0:T(512)}, u32[]{:S(2)}) copy-start(f32[512]{0:T(512)} %get-tuple-element.10) | copy-start | bytes 6148
  539.9 19.9 %copy-start.86 = (f32[512]{0:T(512)S(1)}, f32[512]{0:T(512)}, u32[]{:S(2)}) copy-start(f32[512]{0:T(512)} %get-tuple-element.17) | copy-start | bytes 6148
  539.9 19.9 %copy-start.95 = (f32[512]{0:T(512)S(1)}, f32[512]{0:T(512)}, u32[]{:S(2)}) copy-start(f32[512]{0:T(512)} %get-tuple-element.50) | copy-start | bytes 6148
  540.0 19.9 %copy-start.96 = (f32[512]{0:T(512)S(1)}, f32[512]{0:T(512)}, u32[]{:S(2)}) copy-start(f32[512]{0:T(512)} %get-tuple-element.120) | copy-start | bytes 6148
  540.0 62.1 %copy-start.68 = (f32[11,512]{1,0:T(8,128)S(1)}, f32[11,512]{1,0:T(8,128)}, u32[]{:S(2)}) copy-start(f32[11,512]{1,0:T(8,128)} %param.15) | copy-start | bytes 67588
  540.0 62.1 %copy-start.77 = (f32[11,512]{1,0:T(8,128)S(1)}, f32[11,512]{1,0:T(8,128)}, u32[]{:S(2)}) copy-start(f32[11,512]{1,0:T(8,128)} %param.17) | copy-start | bytes 67588
  540.0 62.0 %copy-start.78 = (f32[11,512]{1,0:T(8,128)S(1)}, f32[11,512]{1,0:T(8,128)}, u32[]{:S(2)}) copy-start(f32[11,512]{1,0:T(8,128)} %param.16) | copy-start | bytes 67588
  540.0 62.7 %copy-start.5 = (f32[4,8,32,512]{3,2,1,0:T(8,128)S(1)}, f32[4,8,32,512]{3,2,1,0:T(8,128)}, u32[]{:S(2)}) copy-start(f32[4,8,32,512]{3,2,1,0:T(8,128)} %copy-done.4) | copy-start | bytes 6291460
  602.0 4.6 copy-start.66
  (52 other events, 84.0 us)
Sparse Core Ops, SparseCore 0:
  11.5 93.8 all-gather.4
  209.6 33.9 all-gather.8
  245.2 34.4 all-gather.6
  282.1 44.5 reduce-scatter.4
  329.2 44.5 reduce-scatter.2
  503.9 368.5 all-reduce.12
where the time goes:
time: 894 us; the launch traced here: 883 us
  waiting for transfers between devices  418 us (47%)
  local copies, waits for them, and re-layouts  162 us (18%)
  matrix products  120 us (13%)
  blocking collectives  91.4 us (10%)
  other arithmetic  63.5 us (7%)
  between operations  15.8 us (2%)
  starting transfers between devices  12 us (1%)
    unnamed x7, waiting for transfers between devices  266 us
    all_gather x1, waiting for transfers between devices, per_device(): lax.all_gather(matrix_weight.astype(jnp.bfloat16), ('img', 'band'), axis=...  75.9 us
    unnamed x208, local copies, waits for them, and re-layouts  52.9 us
    dot_general x36, matrix products, taps(): jnp.einsum('ghwc,cd->ghwd', padded[:, row:row + height, column:column + w...  50.1 us
    psum x1, blocking collectives, per_device(): vector_grads = lax.psum(vector_terms, ('img', 'band'))  42.1 us
    slice x18, local copies, waits for them, and re-layouts, taps(): kernel[tap]  34.8 us
    all_gather x1, waiting for transfers between devices, per_device(): lax.all_gather(key_low, 'band', axis=1, tiled=True)  27.7 us
    psum x3, blocking collectives, normalize_back(): grad_sums = lax.psum(grad_sums, 'band')  25.8 us
  transfers between devices with their start and end apart: 14, of which 7 were waited for; matrix products, arithmetic and copies ran while one was open for 21% of the time, Pallas kernels for 0%

commit v1 on v0

--- a/solution.py
+++ b/solution.py
@@ -1,6 +1,8 @@
 import jax
 import jax.numpy as jnp
 from jax import lax
+from jax.experimental import pallas as pl
+from jax.experimental.pallas import tpu as pltpu
 from jax.sharding import PartitionSpec as P
 
 GROUPS = 32
@@ -127,7 +129,7 @@
     return (raised / total, top, total)
 
 
-def per_device(
+def banded(
     images,
     cotangent,
     sizes,
@@ -308,9 +310,560 @@
     )
 
 
+F32 = jnp.float32
+BF16 = jnp.bfloat16
+SIDE = 32
+VMEM_LIMIT = 58 * 1024 * 1024
+
+
+def dot(a, b):
+    return lax.dot_general(a, b, (((1,), (0,)), ((), ())), preferred_element_type=F32)
+
+
+def dot_nt(a, b):
+    return lax.dot_general(a, b, (((1,), (1,)), ((), ())), preferred_element_type=F32)
+
+
+def dot_tn(a, b):
+    return lax.dot_general(a, b, (((0,), (0,)), ((), ())), preferred_element_type=F32)
+
+
+def call(body, outs, ins, scratch=(), flops=0, name=None):
+    spaces = {"v": pl.BlockSpec(memory_space=pltpu.VMEM), "s": pl.BlockSpec(memory_space=pltpu.SMEM),
+              "a": pl.BlockSpec(memory_space=pl.ANY)}
+    moved = sum(a.size * a.dtype.itemsize for a, _ in ins) + sum(
+        o.size * o.dtype.itemsize for o, _ in outs)
+    return pl.pallas_call(
+        body,
+        out_shape=[o for o, _ in outs],
+        in_specs=[spaces[s] for _, s in ins],
+        out_specs=[spaces[s] for _, s in outs],
+        scratch_shapes=list(scratch),
+        compiler_params=pltpu.CompilerParams(vmem_limit_bytes=VMEM_LIMIT),
+        cost_estimate=pl.CostEstimate(flops=flops, bytes_accessed=moved, transcendentals=0),
+        name=name,
+    )(*[a for a, _ in ins])
+
+
+def shape(dims, dtype):
+    return jax.ShapeDtypeStruct(dims, dtype)
+
+
+def fold(x):
+    return jnp.sum(x.reshape(x.shape[0] // 8, 8, x.shape[1]), axis=0)
+
+
+def group_total(x):
+    lane = lax.broadcasted_iota(jnp.int32, x.shape, 1)
+    width = x.shape[1]
+    for s in (1, 2, 4, 8):
+        up = pltpu.roll(x, width - s, 1)
+        down = pltpu.roll(x, s, 1)
+        x = x + jnp.where((lane & s) == 0, up, down)
+    return x
+
+
+def total_of(*parts):
+    rows = [jnp.sum(p, axis=0, keepdims=True) for p in parts]
+    pad = jnp.zeros((8 - len(rows), rows[0].shape[1]), F32)
+    return jnp.concatenate(rows + [pad], axis=0)
+
+
+def moments(s1, s2, size):
+    count = (size * size * 16).astype(F32)
+    both = group_total(total_of(s1, s2)) / count
+    mean = both[0:1]
+    spread = both[1:2] - mean * mean
+    return mean, lax.rsqrt(spread + EPS)
+
+
+def row_mask(size, channels):
+    across = lax.broadcasted_iota(jnp.int32, (SIDE, channels), 0)
+    inside = across < size
+    return lambda h: inside & (h < size)
+
+
+def sigmoid(y):
+    return 0.5 * jnp.tanh(0.5 * y) + 0.5
+
+
+def rows(h):
+    return pl.ds(pl.multiple_of(h * SIDE, SIDE), SIDE)
+
+
+def put_shifted(ref, h, r, forward):
+    channels = r.shape[1]
+    w = lax.broadcasted_iota(jnp.int32, r.shape, 0)
+    before = jnp.where(w == 0, 0.0, pltpu.roll(r, 1, 0)).astype(BF16)
+    after = jnp.where(w == SIDE - 1, 0.0, pltpu.roll(r, SIDE - 1, 0)).astype(BF16)
+    first, last = (before, after) if forward else (after, before)
+    at = pl.ds(pl.multiple_of((h + 1) * SIDE, SIDE), SIDE)
+    ref[at, 0:channels] = first
+    ref[at, channels : 2 * channels] = r.astype(BF16)
+    ref[at, 2 * channels :] = last
+
+
+def clear_border(ref):
+    zero = jnp.zeros((SIDE, ref.shape[1]), BF16)
+    ref[0:SIDE, :] = zero
+    ref[(SIDE + 1) * SIDE :, :] = zero
+
+
+def put_transposed(ref, src_ref, row0, lane0):
+    channels, count = ref.shape
+    for j in range(count // 256):
+        block = src_ref[row0 + j * 256 : row0 + (j + 1) * 256, lane0 : lane0 + channels]
+        ref[:, j * 256 : (j + 1) * 256] = block.T
+
+
+def act_one_body(size_ref, img_ref, vec_ref, a3_ref, at_ref, stat_ref):
+    size = size_ref[0]
+    channels = img_ref.shape[1]
+    mask = row_mask(size, channels)
+
+    def sums(h, carry):
+        x = jnp.where(mask(h), img_ref[rows(h), :].astype(F32), 0.0)
+        return carry[0] + fold(x), carry[1] + fold(x * x)
+
+    zero = jnp.zeros((8, channels), F32)
+    s1, s2 = lax.fori_loop(0, SIDE, sums, (zero, zero), unroll=2)
+    mean, scale = moments(s1, s2, size)
+    stat_ref[0:1, :] = mean
+    stat_ref[1:2, :] = scale
+    stat_ref[2:8, :] = jnp.zeros((6, channels), F32)
+    apply_norm(img_ref, mean, scale * vec_ref[0:1, :], vec_ref[1:2, :], mask, a3_ref)
+    put_transposed(at_ref, a3_ref, SIDE, channels)
+
+
+def apply_norm(src_ref, mean, scale, shift, mask, a3_ref):
+    clear_border(a3_ref)
+
+    def apply(h, carry):
+        y = (src_ref[rows(h), :].astype(F32) - mean) * scale + shift
+        r = jnp.where(mask(h), y * sigmoid(y), 0.0).astype(BF16).astype(F32)
+        put_shifted(a3_ref, h, r, True)
+        return carry
+
+    lax.fori_loop(0, SIDE, apply, 0, unroll=2)
+
+
+def act_one(size, img, vec):
+    n, c = img.shape
+    return call(act_one_body,
+        [(shape((n + 64, 3 * c), BF16), "v"), (shape((c, n), BF16), "v"), (shape((8, c), F32), "v")],
+        [(size, "s"), (img, "v"), (vec, "v")], name="act_one")
+
+
+MB = 512
+
+
+def start_copies(src_ref, dst_ref, sems, parts, offset=0):
+    length = dst_ref.shape[0] // parts
+    copies = [
+        pltpu.make_async_copy(src_ref.at[pl.ds(offset + p * length, length)], dst_ref.at[pl.ds(p * length, length)], sems.at[p])
+        for p in range(parts)
+    ]
+    for copy in copies:
+        copy.start()
+    return copies
+
+
+def conv(a3_ref, k_ref, copies, out_ref, finish):
+    n, c = out_ref.shape
+    depth = 3 * c
+    for dy in range(3):
+        copies[dy].wait()
+        kernel = k_ref[dy * depth : (dy + 1) * depth, :]
+
+        def block(m, carry):
+            at = pl.multiple_of(m * MB, MB)
+            value = dot(a3_ref[pl.ds(at + dy * SIDE, MB), :], kernel)
+            if dy > 0:
+                value = value + out_ref[pl.ds(at, MB), :]
+            if dy == 2:
+                value = finish(at, value)
+            out_ref[pl.ds(at, MB), :] = value
+            return carry
+
+        lax.fori_loop(0, n // MB, block, 0, unroll=True)
+
+
+def conv_one_body(size_ref, a3_ref, k_ref, vec_ref, conv_ref, a3_out, at_out, stat_ref, k_vmem, sems):
+    copies = start_copies(k_ref, k_vmem, sems, 3)
+    size = size_ref[0]
+    channels = conv_ref.shape[1]
+    mask = row_mask(size, channels)
+    bias = vec_ref[2:3, :]
+    conv(a3_ref, k_vmem, copies, conv_ref, lambda at, v: v + bias)
+
+    def sums(h, carry):
+        x = jnp.where(mask(h), conv_ref[rows(h), :], 0.0)
+        return carry[0] + fold(x), carry[1] + fold(x * x)
+
+    zero = jnp.zeros((8, channels), F32)
+    s1, s2 = lax.fori_loop(0, SIDE, sums, (zero, zero), unroll=2)
+    mean, scale = moments(s1, s2, size)
+    stat_ref[0:1, :] = mean
+    stat_ref[1:2, :] = scale
+    stat_ref[2:8, :] = jnp.zeros((6, channels), F32)
+    apply_norm(conv_ref, mean, scale * vec_ref[3:4, :], vec_ref[4:5, :], mask, a3_out)
+    put_transposed(at_out, a3_out, SIDE, channels)
+
+
+def conv_one(size, a3, weights, vec):
+    n, c = a3.shape[0] - 64, a3.shape[1] // 3
+    return call(conv_one_body,
+        [(shape((n, c), F32), "v"), (shape((n + 64, 3 * c), BF16), "v"), (shape((c, n), BF16), "v"), (shape((8, c), F32), "v")],
+        [(size, "s"), (a3, "v"), (weights, "a"), (vec, "v")],
+        [pltpu.VMEM((9 * c, c), BF16), pltpu.SemaphoreType.DMA((3,))],
+        flops=2 * n * 9 * c * c, name="conv_one")
+
+
+def conv_two_body(size_ref, a3_ref, k_ref, vec_ref, img_ref, resid_ref, normed_ref, stat_ref, k_vmem, sems):
+    channels = resid_ref.shape[1]
+    copies = start_copies(k_ref, k_vmem, sems, 3, 9 * channels)
+    size = size_ref[0]
+    mask = row_mask(size, channels)
+    bias = vec_ref[5:6, :]
+    conv(a3_ref, k_vmem, copies, resid_ref, lambda at, v: v + bias + img_ref[pl.ds(at, MB), :].astype(F32))
+
+    def sums(h, carry):
+        x = jnp.where(mask(h), resid_ref[rows(h), :], 0.0)
+        resid_ref[rows(h), :] = x
+        return carry[0] + fold(x), carry[1] + fold(x * x)
+
+    zero = jnp.zeros((8, channels), F32)
+    s1, s2 = lax.fori_loop(0, SIDE, sums, (zero, zero), unroll=2)
+    mean, scale = moments(s1, s2, size)
+    stat_ref[0:1, :] = mean
+    stat_ref[1:2, :] = scale
+    stat_ref[2:8, :] = jnp.zeros((6, channels), F32)
+    gain = scale * vec_ref[6:7, :]
+    shift = vec_ref[7:8, :]
+
+    def apply(h, carry):
+        y = (resid_ref[rows(h), :] - mean) * gain + shift
+        normed_ref[rows(h), :] = jnp.where(mask(h), y, 0.0).astype(BF16)
+        return carry
+
+    lax.fori_loop(0, SIDE, apply, 0, unroll=2)
+
+
+def conv_two(size, a3, weights, vec, img):
+    n, c = img.shape
+    return call(conv_two_body,
+        [(shape((n, c), F32), "v"), (shape((n, c), BF16), "v"), (shape((8, c), F32), "v")],
+        [(size, "s"), (a3, "v"), (weights, "a"), (vec, "v"), (img, "v")],
+        [pltpu.VMEM((9 * c, c), BF16), pltpu.SemaphoreType.DMA((3,))],
+        flops=2 * n * 9 * c * c, name="conv_two")
+
+
+QB = 256
+
+
+def attention_body(size_ref, normed_ref, w_ref, vec_ref, resid_ref, cot_ref, stat_ref,
+                   out_ref, gw_ref, grad_ref, e3_ref, vout_ref,
+                   w_vmem, q_ref, k_ref, v_ref, p_ref, ds_ref, mixed_ref, top_ref, gm_ref, gq_ref, gk_ref, gv_ref, nt_ref, sems):
+    n, c = normed_ref.shape
+    copies = start_copies(w_ref, w_vmem, sems, 4, 18 * c)
+    size = size_ref[0]
+    mask = row_mask(size, c)
+    factor = c ** (-0.5)
+
+    def top_rows(h, carry):
+        t = jnp.where(mask(h), cot_ref[rows(h), :].astype(F32), 0.0)
+        top_ref[rows(h), :] = t.astype(BF16)
+        return carry + fold(t)
+
+    zero = jnp.zeros((8, c), F32)
+    top_sum = lax.fori_loop(0, SIDE, top_rows, zero, unroll=2)
+    put_transposed(nt_ref, normed_ref, 0, 0)
+    for j in range(4):
+        copies[j].wait()
+    wq, wk, wv, wo = (w_vmem[j * c : (j + 1) * c, :] for j in range(4))
+    qb, vb, ob = (vec_ref[j : j + 1, :] for j in (8, 9, 10))
+
+    for m in range(n // MB):
+        at = slice(m * MB, (m + 1) * MB)
+        x = normed_ref[at, :]
+        q_ref[at, :] = (dot(x, wq) + qb).astype(BF16)
+        k_ref[at, :] = dot(x, wk).astype(BF16)
+        v_ref[at, :] = (dot(x, wv) + vb).astype(BF16)
+        gm_ref[at, :] = dot_nt(top_ref[at, :], wo).astype(BF16)
+
+    spot = lax.broadcasted_iota(jnp.int32, (QB, n), 1)
+    key_valid = ((spot >> 5) < size) & ((spot & 31) < size)
+
+    def queries(m, carry):
+        at = pl.ds(pl.multiple_of(m * QB, QB), QB)
+        s = dot_nt(q_ref[at, :], k_ref[...]) * factor
+        s = jnp.where(key_valid, s, -1e30)
+        raised = jnp.exp(s - jnp.max(s, axis=1, keepdims=True))
+        p = raised / jnp.sum(raised, axis=1, keepdims=True)
+        low = p.astype(BF16)
+        p_ref[at, :] = low
+        mixed_ref[at, :] = dot(low, v_ref[...]).astype(BF16)
+        gp = dot_nt(gm_ref[at, :], v_ref[...])
+        weighted = jnp.sum(p * gp, axis=1, keepdims=True)
+        ds = (p * (gp - weighted) * factor).astype(BF16)
+        ds_ref[at, :] = ds
+        gq_ref[at, :] = dot(ds, k_ref[...]).astype(BF16)
+        return carry
+
+    lax.fori_loop(0, n // QB, queries, 0)
+
+    def keys(m, carry):
+        at = pl.ds(pl.multiple_of(m * QB, QB), QB)
+        gk_ref[at, :] = dot_tn(ds_ref[:, at], q_ref[...]).astype(BF16)
+        gv_ref[at, :] = dot_tn(p_ref[:, at], gm_ref[...]).astype(BF16)
+        return carry
+
+    lax.fori_loop(0, n // QB, keys, 0)
+
+    gw_ref[0:c, :] = dot(nt_ref[...], gq_ref[...]).astype(gw_ref.dtype)
+    gw_ref[c : 2 * c, :] = dot(nt_ref[...], gk_ref[...]).astype(gw_ref.dtype)
+    gw_ref[2 * c : 3 * c, :] = dot(nt_ref[...], gv_ref[...]).astype(gw_ref.dtype)
+    gw_ref[3 * c : 4 * c, :] = dot_tn(mixed_ref[...], top_ref[...]).astype(gw_ref.dtype)
+
+    for m in range(n // MB):
+        at = slice(m * MB, (m + 1) * MB)
+        grad_ref[at, :] = dot_nt(gq_ref[at, :], wq) + dot_nt(gk_ref[at, :], wk) + dot_nt(gv_ref[at, :], wv)
+
+    mean, scale = stat_ref[0:1, :], stat_ref[1:2, :]
+
+    def sums(h, carry):
+        u = jnp.where(mask(h), grad_ref[rows(h), :], 0.0)
+        xhat = (resid_ref[rows(h), :] - mean) * scale
+        gq = fold(gq_ref[rows(h), :].astype(F32))
+        gv = fold(gv_ref[rows(h), :].astype(F32))
+        return carry[0] + fold(u), carry[1] + fold(u * xhat), carry[2] + gq, carry[3] + gv
+
+    su, sux, sq, sv = lax.fori_loop(0, SIDE, sums, (zero, zero, zero, zero), unroll=2)
+    count = (size * size * 16).astype(F32)
+    gain = vec_ref[6:7, :]
+    channel = total_of(su, sux)
+    both = group_total(channel * gain) / count
+    m1, m2 = both[0:1], both[1:2]
+    clear_border(e3_ref)
+
+    def apply(h, carry):
+        xhat = (resid_ref[rows(h), :] - mean) * scale
+        g = (grad_ref[rows(h), :] * gain - m1 - xhat * m2) * scale + top_ref[rows(h), :].astype(F32)
+        g = jnp.where(mask(h), g, 0.0)
+        grad_ref[rows(h), :] = g
+        put_shifted(e3_ref, h, g.astype(BF16).astype(F32), False)
+        return carry + fold(g)
+
+    sg = lax.fori_loop(0, SIDE, apply, zero, unroll=2)
+    vout_ref[...] = total_of(sg, su * 0.0 + sux, su, sq, sv, top_sum)
+
+    for m in range(n // MB):
+        at = slice(m * MB, (m + 1) * MB)
+        out_rows = dot(mixed_ref[at, :], wo) + ob + resid_ref[at, :]
+        place = lax.broadcasted_iota(jnp.int32, (MB, c), 0) + m * MB
+        good = ((place >> 5) < size) & ((place & 31) < size)
+        out_ref[at, :] = jnp.where(good, out_rows, 0.0).astype(BF16)
+
+
+def attention(size, normed, weights, vec, resid, cot, stat):
+    n, c = normed.shape
+    full, wide = pltpu.VMEM((n, c), BF16), pltpu.VMEM((n, n), BF16)
+    return call(attention_body,
+        [(shape((n, c), BF16), "v"), (shape((4 * c, c), BF16), "v"), (shape((n, c), F32), "v"),
+         (shape((n + 64, 3 * c), BF16), "v"), (shape((8, c), F32), "v")],
+        [(size, "s"), (normed, "v"), (weights, "a"), (vec, "v"), (resid, "v"), (cot, "v"), (stat, "v")],
+        [pltpu.VMEM((4 * c, c), BF16), full, full, full, wide, wide, full, full, full, full, full, full,
+         pltpu.VMEM((c, n), BF16), pltpu.SemaphoreType.DMA((4,))],
+        flops=2 * n * c * (12 * c + 7 * n), name="attention")
+
+
+def grad_kernel_body(e3_ref, at_ref, gk_ref, stage, sems):
+    c, n = at_ref.shape
+    copies = []
+    for dy in range(3):
+        for dx in range(3):
+            tap = 3 * dy + dx
+            lo = (2 - dy) * SIDE
+            value = dot(at_ref[...], e3_ref[lo : lo + n, dx * c : (dx + 1) * c])
+            stage[tap * c : (tap + 1) * c, :] = value.astype(gk_ref.dtype)
+            copy = pltpu.make_async_copy(stage.at[pl.ds(tap * c, c)], gk_ref.at[pl.ds(tap * c, c)], sems.at[tap])
+            copy.start()
+            copies.append(copy)
+    for copy in copies:
+        copy.wait()
+
+
+def grad_kernel(e3, at, name):
+    c, n = at.shape
+    return call(grad_kernel_body, [(shape((9 * c, c), BF16), "a")], [(e3, "v"), (at, "v")],
+        [pltpu.VMEM((9 * c, c), BF16), pltpu.SemaphoreType.DMA((9,))],
+        flops=2 * n * 9 * c * c, name=name)[0]
+
+
+def conv_back(e3_ref, k_ref, copies, out_ref):
+    n, c = out_ref.shape
+    for dy in range(3):
+        copies[dy].wait()
+        lo = (2 - dy) * SIDE
+        for m in range(n // MB):
+            value = None
+            for dx in range(3):
+                tap = 3 * dy + dx
+                term = dot_nt(e3_ref[lo + m * MB : lo + (m + 1) * MB, dx * c : (dx + 1) * c], k_ref[tap * c : (tap + 1) * c, :])
+                value = term if value is None else value + term
+            if dy > 0:
+                value = value + out_ref[m * MB : (m + 1) * MB, :]
+            out_ref[m * MB : (m + 1) * MB, :] = value
+
+
+def norm_back_sums(src_ref, g_ref, mean, scale, gain, shift, mask, size):
+    c = g_ref.shape[1]
+
+    def sums(h, carry):
+        xhat = (src_ref[rows(h), :].astype(F32) - mean) * scale
+        y = xhat * gain + shift
+        s = sigmoid(y)
+        u = jnp.where(mask(h), g_ref[rows(h), :] * (s * (1.0 + y * (1.0 - s))), 0.0)
+        g_ref[rows(h), :] = u
+        return carry[0] + fold(u), carry[1] + fold(u * xhat)
+
+    zero = jnp.zeros((8, c), F32)
+    su, sux = lax.fori_loop(0, SIDE, sums, (zero, zero), unroll=2)
+    count = (size * size * 16).astype(F32)
+    both = group_total(total_of(su, sux) * gain) / count
+    return su, sux, both[0:1], both[1:2]
+
+
+def back_two_body(size_ref, e3_ref, k_ref, vec_ref, conv_ref, stat_ref, e3_out, vout_ref, g_ref, k_vmem, sems):
+    n, c = conv_ref.shape
+    copies = start_copies(k_ref, k_vmem, sems, 3, 9 * c)
+    size = size_ref[0]
+    mask = row_mask(size, c)
+    conv_back(e3_ref, k_vmem, copies, g_ref)
+    mean, scale = stat_ref[0:1, :], stat_ref[1:2, :]
+    gain, shift = vec_ref[3:4, :], vec_ref[4:5, :]
+    su, sux, m1, m2 = norm_back_sums(conv_ref, g_ref, mean, scale, gain, shift, mask, size)
+    clear_border(e3_out)
+
+    def apply(h, carry):
+        xhat = (conv_ref[rows(h), :] - mean) * scale
+        g = jnp.where(mask(h), (g_ref[rows(h), :] * gain - m1 - xhat * m2) * scale, 0.0)
+        put_shifted(e3_out, h, g.astype(BF16).astype(F32), False)
+        return carry + fold(g)
+
+    sg = lax.fori_loop(0, SIDE, apply, jnp.zeros((8, c), F32), unroll=2)
+    vout_ref[...] = total_of(sg, sux, su)
+
+
+def back_two(size, e3, weights, vec, conv_out, stat):
+    n, c = conv_out.shape
+    return call(back_two_body, [(shape((n + 64, 3 * c), BF16), "v"), (shape((8, c), F32), "v")],
+        [(size, "s"), (e3, "v"), (weights, "a"), (vec, "v"), (conv_out, "v"), (stat, "v")],
+        [pltpu.VMEM((n, c), F32), pltpu.VMEM((9 * c, c), BF16), pltpu.SemaphoreType.DMA((3,))],
+        flops=2 * n * 9 * c * c, name="back_two")
+
+
+def back_one_body(size_ref, e3_ref, k_ref, vec_ref, img_ref, stat_ref, resid_ref, out_ref, vout_ref, g_ref, k_vmem, sems):
+    n, c = img_ref.shape
+    copies = start_copies(k_ref, k_vmem, sems, 3)
+    size = size_ref[0]
+    mask = row_mask(size, c)
+    conv_back(e3_ref, k_vmem, copies, g_ref)
+    mean, scale = stat_ref[0:1, :], stat_ref[1:2, :]
+    gain, shift = vec_ref[0:1, :], vec_ref[1:2, :]
+    su, sux, m1, m2 = norm_back_sums(img_ref, g_ref, mean, scale, gain, shift, mask, size)
+
+    def apply(h, carry):
+        xhat = (img_ref[rows(h), :].astype(F32) - mean) * scale
+        g = (g_ref[rows(h), :] * gain - m1 - xhat * m2) * scale + resid_ref[rows(h), :]
+        out_ref[rows(h), :] = jnp.where(mask(h), g, 0.0).astype(out_ref.dtype)
+        return carry
+
+    lax.fori_loop(0, SIDE, apply, 0, unroll=2)
+    vout_ref[...] = total_of(sux, su)
+
+
+def back_one(size, e3, weights, vec, img, stat, grad_resid):
+    n, c = img.shape
+    return call(back_one_body, [(shape((n, c), BF16), "v"), (shape((8, c), F32), "v")],
+        [(size, "s"), (e3, "v"), (weights, "a"), (vec, "v"), (img, "v"), (stat, "v"), (grad_resid, "v")],
+        [pltpu.VMEM((n, c), F32), pltpu.VMEM((9 * c, c), BF16), pltpu.SemaphoreType.DMA((3,))],
+        flops=2 * n * 9 * c * c, name="back_one")
+
+
+ALL = ("img", "band")
+
+
+def whole_image(
+    images,
+    cotangent,
+    sizes,
+    matrix_weight,
+    matrix_momentum,
+    matrix_average,
+    vector_weight,
+    vector_momentum,
+    vector_average,
+):
+    batch, height, width, c = images.shape
+    n = width * width
+    mine = lax.axis_index("band")
+    size = lax.dynamic_slice_in_dim(sizes, mine, 1)
+
+    def to_image(field):
+        parts = field.reshape(batch, height * width, c)
+        return lax.all_to_all(parts, "band", 0, 0, tiled=True).reshape(n, c)
+
+    def to_bands(field):
+        parts = field.reshape(batch, height * width, c)
+        return lax.all_to_all(parts, "band", 0, 0, tiled=True).reshape(batch, height, width, c)
+
+    weights = lax.all_gather(matrix_weight.astype(BF16).reshape(-1, c), ALL, axis=0, tiled=True)
+    img = to_image(images)
+    cot = to_image(cotangent)
+    a3_one, at_one, stat_one = act_one(size, img, vector_weight)
+    conv_out, a3_two, at_two, stat_two = conv_one(size, a3_one, weights, vector_weight)
+    resid, normed, stat_three = conv_two(size, a3_two, weights, vector_weight, img)
+    out, gw, grad_resid, e3_two, v3 = attention(size, normed, weights, vector_weight, resid, cot, stat_three)
+    gk2 = grad_kernel(e3_two, at_two, "grad_kernel_two")
+    e3_one, v2 = back_two(size, e3_two, weights, vector_weight, conv_out, stat_two)
+    gk1 = grad_kernel(e3_one, at_one, "grad_kernel_one")
+    grad_in, v1 = back_one(size, e3_one, weights, vector_weight, img, stat_one, grad_resid)
+    block_out = to_bands(out)
+    input_grad = to_bands(grad_in).astype(F32)
+    vecs = jnp.stack([v1[0], v1[1], v2[0], v2[1], v2[2], v3[0], v3[1], v3[2], v3[3], v3[4], v3[5]])
+    vector_grads = lax.psum(vecs, ALL)
+    low_grads = lax.psum_scatter(jnp.concatenate([gk1, gk2, gw]), ALL, scatter_dimension=0, tiled=True)
+    matrix_grads = low_grads.astype(F32).reshape(-1)
+    matrix_moments = MOMENTUM * matrix_momentum + matrix_grads
+    matrix_masters = matrix_weight - LR_MATRIX * (matrix_grads + MOMENTUM * matrix_moments)
+    matrix_means = AVERAGE * matrix_average + (1.0 - AVERAGE) * matrix_masters
+    vector_moments = MOMENTUM * vector_momentum + vector_grads
+    vector_masters = vector_weight - LR_VECTOR * (vector_grads + MOMENTUM * vector_moments)
+    vector_means = AVERAGE * vector_average + (1.0 - AVERAGE) * vector_masters
+    return (
+        block_out,
+        input_grad,
+        matrix_grads,
+        matrix_moments,
+        matrix_means,
+        matrix_masters,
+        vector_grads,
+        vector_moments,
+        vector_means,
+        vector_masters,
+    )
+
+
 def solution(mesh):
+    whole = mesh.shape["band"]
+
+    def per_device(images, *rest):
+        step = whole_image if images.shape[0] == whole and SIDE == images.shape[2] else banded
+        return step(images, *rest)
+
     return jax.shard_map(
-        per_device,
+            per_device,
         mesh=mesh,
         in_specs=(
             P("img", "band", None, None),

time: 894 us -> 404 us (0.45); the launches traced: 883 us -> 403 us
  waiting for transfers between devices: 418 us -> 164 us
  local copies, waits for them, and re-layouts: 162 us -> 5.82 us
  matrix products: 120 us -> 0 us
  Pallas kernels: 0 us -> 104 us
  blocking collectives: 91.4 us -> 61.3 us
  other arithmetic: 63.5 us -> 38.7 us
    unnamed x7 -> x2, waiting for transfers between devices: 266 us -> 0.03 us
    dot_general x66 -> x0, matrix products: 120 us -> none  [the longest x36 50.1 us: taps(): jnp.einsum('ghwc,cd->ghwd', padded[:, row:row + height, column:column + w...]
    pallas_call x0 -> x8, Pallas kernels: none -> 104 us  [call(): pl.pallas_call(body, out_shape=[o for o, _ in outs], in_specs=[spaces[s]...]
    slice x34 -> x2, local copies, waits for them, and re-layouts: 94.5 us -> 1.44 us  [the longest x1 0.72 us: whole_image(): v2[0]]
    all_gather x3 -> x1, waiting for transfers between devices: 128 us -> 67.5 us  [whole_image(): lax.all_gather(matrix_weight.astype(BF16).reshape(-1, c), ALL, axis=0, ti...]
    unnamed x208 -> x18, local copies, waits for them, and re-layouts: 52.9 us -> 2.18 us
    reduce_scatter x2 -> x1, waiting for transfers between devices: 18.3 us -> 67.2 us  [whole_image(): lax.psum_scatter(jnp.concatenate([gk1, gk2, gw]), ALL, scatter_dimension=...]
    psum x7 -> x1, blocking collectives: 91.4 us -> 61.3 us  [whole_image(): vector_grads = lax.psum(vecs, ALL)]
  transfers between devices with their start and end apart: 14 -> 6, of which waited for: 7 -> 4; matrix products, arithmetic and copies ran while one was open for 21% -> 2% of each run, Pallas kernels for 0% -> 11%
where the time goes in v1:
time: 404 us; the launch traced here: 403 us
  waiting for transfers between devices  164 us (41%)
  Pallas kernels  104 us (26%)
  blocking collectives  61.3 us (15%)
  other arithmetic  38.7 us (10%)
  starting transfers between devices  14.9 us (4%)
  between operations  14.3 us (4%)
  local copies, waits for them, and re-layouts  5.82 us (1%)
    pallas_call x8, Pallas kernels, call(): pl.pallas_call(body, out_shape=[o for o, _ in outs], in_specs=[spaces[s]...  104 us
    all_gather x1, waiting for transfers between devices, whole_image(): lax.all_gather(matrix_weight.astype(BF16).reshape(-1, c), ALL, axis=0, ti...  67.5 us
    reduce_scatter x1, waiting for transfers between devices, whole_image(): lax.psum_scatter(jnp.concatenate([gk1, gk2, gw]), ALL, scatter_dimension=...  67.2 us
    psum x1, blocking collectives, whole_image(): vector_grads = lax.psum(vecs, ALL)  61.3 us
    concatenate x1, other arithmetic, whole_image(): jnp.concatenate([gk1, gk2, gw])  30 us
    all_to_all x2, waiting for transfers between devices, to_image(): return lax.all_to_all(parts, 'band', 0, 0, tiled=True).reshape(n, c)  15.8 us
    all_to_all x2, waiting for transfers between devices, to_bands(): lax.all_to_all(parts, 'band', 0, 0, tiled=True)  13.4 us
  transfers between devices with their start and end apart: 6, of which 4 were waited for; matrix products, arithmetic and copies ran while one was open for 2% of the time, Pallas kernels for 11%

profile of v1, /device:TPU:0, one launch (start us, length us, event | category | flops | bytes accessed | tf_op | source)
XLA Modules:
  0.0 403.0 jit_solution(6122183529501515948)
XLA Ops:
  7.2 0.0 all-gather.2.cloned.1.call-start
  7.2 1.1 convert_element_type.10
  8.4 1.0 reshape.55
  9.3 0.0 all-gather.2.cloned.1.call-update
  9.4 4.2 %all-to-all-start = ((bf16[4,256,512]{2,1,0:T(8,128)(2,1)}), bf16[4,256,512]{2,1,0:T(8,128)(2,1)S(1)}, u32[]{:S(2)}, u32[]{:S(2)}) async-start(bf16[4,256,512]{2,1,0:T(8,128)(2,1)} %bitcast.22), calls=%async_computation | async-start | bytes 2097152 | tf_op jit(solution)/shard_map/all_to_all | solution.py:815
  13.6 1.2 dynamic_slice.3.size_ref
  14.8 15.8 %all-to-all-done = bf16[4,256,512]{2,1,0:T(8,128)(2,1)S(1)} async-done(((bf16[4,256,512]{2,1,0:T(8,128)(2,1)}), bf16[4,256,512]{2,1,0:T(8,128)(2,1)S(1)}, u32[]{:S(2)}, u32[]{:S(2)}) %all-to-all-start) | async-done | bytes 1048608 | tf_op jit(solution)/shard_map/all_to_all | solution.py:815
  30.6 0.0 copy-start
  30.6 3.5 all-to-all-start.1
  34.2 0.0 reduce-scatter.2.cloned.1.call-start
  34.2 0.0 copy-done
  34.2 6.0 %act_one.1 = (bf16[1088,1536]{1,0:T(8,128)(2,1)}, bf16[512,1024]{1,0:T(8,128)(2,1)}, f32[8,512]{1,0:T(8,128)}) custom-call(s32[1]{0:T(128)} %dynamic_slice.3.size_ref, bf16[1024,512]{1,0:T(8,128)(2,1)} %bitcast.13, f32[11,512]{1,0:T(8,128)} %vec_ref.11), custom_call_target="tpu_custom_call" | custom-call | bytes 5478404 | tf_op jit(solution)/shard_map/act_one/pallas_call | solution.py:336
  40.2 67.5 %all-gather.2.cloned.1.call-done.k_ref.w_ref = bf16[11264,512]{1,0:T(8,128)(2,1)} async-done(((bf16[352,512]{1,0:T(8,128)(2,1)}), bf16[11264,512]{1,0:T(8,128)(2,1)}) %all-gather.2.cloned.1.call-update) | async-done | bytes 11534352 | tf_op jit(solution)/shard_map/all_gather | solution.py:821
  107.7 13.8 %conv_one.1 = (f32[1024,512]{1,0:T(8,128)}, bf16[1088,1536]{1,0:T(8,128)(2,1)}, bf16[512,1024]{1,0:T(8,128)(2,1)}, f32[8,512]{1,0:T(8,128)}) custom-call(s32[1]{0:T(128)} %dynamic_slice.3.size_ref, bf16[1088,1536]{1,0:T(8,128)(2,1)} %get-tuple-element.29.a3_ref, bf16[11264,512]{1,0:T(8,128)(2,1)} %all-gather.2.cloned.1.call-done.k_ref.w_ref, f32[11,512]{1,0:T(8,128)} %vec_ref.11), custom_call_target="tpu_custom_call" | custom-call | flops 4831838208 | bytes 21403652 | tf_op jit(solution)/shard_map/conv_one/pallas_call | solution.py:336
  121.5 12.3 %conv_two.1 = (f32[1024,512]{1,0:T(8,128)}, bf16[1024,512]{1,0:T(8,128)(2,1)}, f32[8,512]{1,0:T(8,128)}) custom-call(s32[1]{0:T(128)} %dynamic_slice.3.size_ref, bf16[1088,1536]{1,0:T(8,128)(2,1)} %get-tuple-element.30.a3_ref, bf16[11264,512]{1,0:T(8,128)(2,1)} %all-gather.2.cloned.1.call-done.k_ref.w_ref, f32[11,512]{1,0:T(8,128)} %vec_ref.11, ...), custom_call_target="tpu_custom_call" | custom-call | flops 4831838208 | bytes 19109892 | tf_op jit(solution)/shard_map/conv_two/pallas_call | solution.py:336
  133.8 0.0 all-to-all-done.1
  133.8 0.0 copy-start.3
  133.8 1.0 copy-done.3
  134.8 26.8 %attention.1 = (bf16[1024,512]{1,0:T(8,128)(2,1)}, bf16[2048,512]{1,0:T(8,128)(2,1)}, f32[1024,512]{1,0:T(8,128)}, bf16[1088,1536]{1,0:T(8,128)(2,1)}, f32[8,512]{1,0:T(8,128)}) custom-call(s32[1]{0:T(128)} %dynamic_slice.3.size_ref, bf16[1024,512]{1,0:T(8,128)(2,1)} %get-tuple-element.31.normed_ref, ...), custom_call_target="tpu_custom_call" | custom-call | flops 13958643712 | bytes 24369156 | tf_op jit(solution)/shard_map/attention/pallas_call | solution.py:336
  161.7 8.2 %grad_kernel_two.1 = bf16[4608,512]{1,0:T(8,128)(2,1)} custom-call(bf16[1088,1536]{1,0:T(8,128)(2,1)} %get-tuple-element.35.e3_ref, bf16[512,1024]{1,0:T(8,128)(2,1)} %get-tuple-element.43.at_ref), custom_call_target="tpu_custom_call" | custom-call | flops 4831838208 | bytes 9109504 | tf_op jit(solution)/shard_map/grad_kernel_two/pallas_call | solution.py:336
  169.9 0.0 slice-start
  169.9 14.9 %back_two.1 = (bf16[1088,1536]{1,0:T(8,128)(2,1)}, f32[8,512]{1,0:T(8,128)}) custom-call(s32[1]{0:T(128)} %dynamic_slice.3.size_ref, bf16[1088,1536]{1,0:T(8,128)(2,1)} %get-tuple-element.35.e3_ref, bf16[11264,512]{1,0:T(8,128)(2,1)} %all-gather.2.cloned.1.call-done.k_ref.w_ref, f32[11,512]{1,0:T(8,128)} %vec_ref.11, ...), custom_call_target="tpu_custom_call" | custom-call | flops 4831838208 | bytes 20371460 | tf_op jit(solution)/shard_map/back_two/pallas_call | solution.py:336
  184.8 0.0 slice-start.1
  184.8 8.2 %grad_kernel_one.1 = bf16[4608,512]{1,0:T(8,128)(2,1)} custom-call(bf16[1088,1536]{1,0:T(8,128)(2,1)} %get-tuple-element.38.e3_ref, bf16[512,1024]{1,0:T(8,128)(2,1)} %get-tuple-element.42.at_ref), custom_call_target="tpu_custom_call" | custom-call | flops 4831838208 | bytes 9109504 | tf_op jit(solution)/shard_map/grad_kernel_one/pallas_call | solution.py:336
  193.0 0.0 slice-done
  193.0 0.0 slice-done.1
  193.1 30.0 %pad_maximum_fusion = bf16[11264,512]{1,0:T(8,128)(2,1)} fusion(bf16[2048,512]{1,0:T(8,128)(2,1)} %get-tuple-element.44, bf16[4608,512]{1,0:T(8,128)(2,1)S(1)} %bitcast.17, bf16[4608,512]{1,0:T(8,128)(2,1)} %grad_kernel_one.1), kind=kLoop, calls=%fused_computation | loop fusion | flops 34603008 | bytes 23068672 | tf_op jit(solution)/shard_map/concatenate | solution.py:836
  223.0 0.0 reduce-scatter.2.cloned.1.call-update
  223.0 3.5 all-to-all-start.2
  226.6 0.0 copy-start.5
  226.6 13.9 %back_one.1 = (bf16[1024,512]{1,0:T(8,128)(2,1)}, f32[8,512]{1,0:T(8,128)}) custom-call(s32[1]{0:T(128)} %dynamic_slice.3.size_ref, bf16[1088,1536]{1,0:T(8,128)(2,1)} %get-tuple-element.38.e3_ref, bf16[11264,512]{1,0:T(8,128)(2,1)} %all-gather.2.cloned.1.call-done.k_ref.w_ref, f32[11,512]{1,0:T(8,128)} %vec_ref.11, bf16[1024,512]{1,0:T(8,128)(2,1)} %bitcast.15, ...), custom_call_target="tpu_custom_call" | custom-call | flops 4831838208 | bytes 19126276 | tf_op jit(solution)/shard_map/back_one/pallas_call | solution.py:336
  240.5 0.0 copy-start.1
  240.5 0.0 copy-start.4
  240.5 13.4 %all-to-all-done.2 = bf16[4,256,512]{2,1,0:T(8,128)(2,1)S(1)} async-done(((bf16[4,256,512]{2,1,0:T(8,128)(2,1)}), bf16[4,256,512]{2,1,0:T(8,128)(2,1)S(1)}, u32[]{:S(2)}, u32[]{:S(2)}) %all-to-all-start.2) | async-done | bytes 1048608 | tf_op jit(solution)/shard_map/all_to_all | solution.py:819
  253.9 3.5 all-to-all-start.3
  257.4 0.7 slice.10
  258.1 0.7 slice.9
  258.8 0.0 copy-done.5
  258.8 0.6 pad_maximum_fusion.1
  259.5 61.3 %psum.7 = f32[11,512]{1,0:T(8,128)} all-reduce(f32[11,512]{1,0:T(8,128)} %pad_maximum_fusion.1), channel_id=1, replica_groups=mesh['img'=8,'band'=4] {'img','band'}, use_global_device_ids=true, to_apply=%region_1.0 | all-reduce | flops 5632 | bytes 45056 | tf_op jit(solution)/shard_map/psum | solution.py:835
  320.8 1.5 multiply_add_fusion.2
  322.2 0.0 all-to-all-done.3
  322.2 1.6 convert.2
  323.8 67.2 %reduce-scatter.2.cloned.1.call-done = bf16[352,512]{1,0:T(8,128)(2,1)} async-done(((bf16[11264,512]{1,0:T(8,128)(2,1)}), bf16[352,512]{1,0:T(8,128)(2,1)}) %reduce-scatter.2.cloned.1.call-update) | async-done | bytes 360464 | tf_op jit(solution)/shard_map/reduce_scatter | solution.py:836
  391.0 1.1 convert_bitcast_fusion
  392.1 0.2 copy.19
  392.3 0.0 copy-start.2
  392.3 0.0 copy-done.1
  392.3 0.0 copy-done.4
  392.3 2.9 multiply_add_fusion
  395.2 1.0 copy.21
  396.2 0.0 copy-done.2
  (1 shorter events, 0.0 us)
Async XLA Ops:
  7.2 100.5 %all-gather.2.cloned.1.call-start = ((), (), s32[]{:S(2)}) async-start(), calls=%async_computation.5 | async-start | bytes 11894784 | tf_op jit(solution)/shard_map/all_gather | solution.py:821
  9.4 21.3 %all-to-all-start = ((bf16[4,256,512]{2,1,0:T(8,128)(2,1)}), bf16[4,256,512]{2,1,0:T(8,128)(2,1)S(1)}, u32[]{:S(2)}, u32[]{:S(2)}) async-start(bf16[4,256,512]{2,1,0:T(8,128)(2,1)} %bitcast.22), calls=%async_computation | async-start | bytes 2097152 | tf_op jit(solution)/shard_map/all_to_all | solution.py:815
  30.6 3.6 copy-start
  30.6 103.2 %all-to-all-start.1 = ((bf16[4,256,512]{2,1,0:T(8,128)(2,1)}), bf16[4,256,512]{2,1,0:T(8,128)(2,1)S(1)}, u32[]{:S(2)}, u32[]{:S(2)}) async-start(bf16[4,256,512]{2,1,0:T(8,128)(2,1)} %bitcast.23), calls=%async_computation.1 | async-start | bytes 2097152 | tf_op jit(solution)/shard_map/all_to_all | solution.py:815
  34.2 356.8 %reduce-scatter.2.cloned.1.call-start = ((), (), s32[]{:S(2)}) async-start(), calls=%async_computation.6 | async-start | bytes 11894784 | tf_op jit(solution)/shard_map/reduce_scatter | solution.py:836
  133.8 1.0 copy-start.3
  169.9 23.2 %slice-start = ((s8[4718592]{0:T(1024)(128)(4,1)}), s8[4194304]{0:T(1024)(128)(4,1)S(1)}, s32[]{:S(2)}) async-start(s8[4718592]{0:T(1024)(128)(4,1)} %bitcast.16), calls=%async_computation.7 | async-start | bytes 8388608
  184.8 8.3 %slice-start.1 = ((s8[4718592]{0:T(1024)(128)(4,1)}), s8[524288]{0:T(1024)(128)(4,1)S(1)}, s32[]{:S(2)}) async-start(s8[4718592]{0:T(1024)(128)(4,1)} %bitcast.16), calls=%async_computation.8 | async-start | bytes 1048576
  223.0 30.8 %all-to-all-start.2 = ((bf16[4,256,512]{2,1,0:T(8,128)(2,1)}), bf16[4,256,512]{2,1,0:T(8,128)(2,1)S(1)}, u32[]{:S(2)}, u32[]{:S(2)}) async-start(bf16[4,256,512]{2,1,0:T(8,128)(2,1)} %bitcast.4), calls=%async_computation.2 | async-start | bytes 2097152 | tf_op jit(solution)/shard_map/all_to_all | solution.py:819
  226.6 32.3 %copy-start.5 = (f32[8,512]{1,0:T(8,128)S(1)}, f32[8,512]{1,0:T(8,128)}, u32[]{:S(2)}) copy-start(f32[8,512]{1,0:T(8,128)} %get-tuple-element.47) | copy-start | bytes 49156
  240.5 151.8 %copy-start.1 = (f32[180224]{0:T(1024)S(1)}, f32[180224]{0:T(1024)}, u32[]{:S(2)}) copy-start(f32[180224]{0:T(1024)} %param.12) | copy-start | bytes 2162692
  240.5 151.8 %copy-start.4 = (f32[180224]{0:T(1024)S(1)}, f32[180224]{0:T(1024)}, u32[]{:S(2)}) copy-start(f32[180224]{0:T(1024)} %param.14) | copy-start | bytes 2162692
  253.9 68.4 %all-to-all-start.3 = ((bf16[4,256,512]{2,1,0:T(8,128)(2,1)}), bf16[4,256,512]{2,1,0:T(8,128)(2,1)S(1)}, u32[]{:S(2)}, u32[]{:S(2)}) async-start(bf16[4,256,512]{2,1,0:T(8,128)(2,1)} %bitcast.25), calls=%async_computation.3 | async-start | bytes 2097152 | tf_op jit(solution)/shard_map/all_to_all | solution.py:819
  392.3 3.9 copy-start.2
Sparse Core Ops, SparseCore 0:
  11.4 96.2 all-gather.1
  223.2 167.8 reduce-scatter.1

commit v2 on v1

--- a/solution.py
+++ b/solution.py
@@ -1,3 +1,5 @@
+import functools
+
 import jax
 import jax.numpy as jnp
 from jax import lax
@@ -328,7 +330,7 @@
     return lax.dot_general(a, b, (((0,), (0,)), ((), ())), preferred_element_type=F32)
 
 
-def call(body, outs, ins, scratch=(), flops=0, name=None):
+def call(body, outs, ins, scratch=(), flops=0, name=None, aliases=None):
     spaces = {"v": pl.BlockSpec(memory_space=pltpu.VMEM), "s": pl.BlockSpec(memory_space=pltpu.SMEM),
               "a": pl.BlockSpec(memory_space=pl.ANY)}
     moved = sum(a.size * a.dtype.itemsize for a, _ in ins) + sum(
@@ -339,6 +341,7 @@
         in_specs=[spaces[s] for _, s in ins],
         out_specs=[spaces[s] for _, s in outs],
         scratch_shapes=list(scratch),
+        input_output_aliases=aliases or {},
         compiler_params=pltpu.CompilerParams(vmem_limit_bytes=VMEM_LIMIT),
         cost_estimate=pl.CostEstimate(flops=flops, bytes_accessed=moved, transcendentals=0),
         name=name,
@@ -558,12 +561,37 @@
         flops=2 * n * 9 * c * c, name="conv_two")
 
 
+def pieces_of(row, count, block):
+    found = []
+    for owner in range(row // block, (row + count - 1) // block + 1):
+        found.append((owner, max(row, owner * block), min(row + count, (owner + 1) * block)))
+    return found
+
+
+def send_rows(stage, base, row, count, at_ref, halves, sem, block):
+    started = []
+    for owner, lo, hi in pieces_of(row, count, block):
+        half, spot = owner // 16, owner % 16
+        z, x, y, c = spot // 8, (spot >> 2) & 1, (spot >> 1) & 1, spot & 1
+        index = ((at_ref[1] ^ x) * 2 + (at_ref[2] ^ y)) * 2 + z
+        source = stage.at[pl.ds(base + lo - row, hi - lo)]
+        place = pl.ds(lo - owner * block, hi - lo)
+        for kept, ref in enumerate(halves[half]):
+
+            @pl.when(((at_ref[3] ^ c) == kept))
+            def _(ref=ref, source=source, place=place):
+                pltpu.make_async_copy(source, ref.at[index, place], sem).start()
+
+    wait = pltpu.make_async_copy(stage.at[pl.ds(base, count)], stage.at[pl.ds(base, count)], sem)
+    return wait
+
+
 QB = 256
 
 
 def attention_body(size_ref, normed_ref, w_ref, vec_ref, resid_ref, cot_ref, stat_ref,
-                   out_ref, gw_ref, grad_ref, e3_ref, vout_ref,
-                   w_vmem, q_ref, k_ref, v_ref, p_ref, ds_ref, mixed_ref, top_ref, gm_ref, gq_ref, gk_ref, gv_ref, nt_ref, sems):
+                   out_ref, mine_ref, theirs_ref, grad_ref, e3_ref, vout_ref,
+                   gw_ref, gw_sem, w_vmem, q_ref, k_ref, v_ref, p_ref, ds_ref, mixed_ref, top_ref, gm_ref, gq_ref, gk_ref, gv_ref, nt_ref, sems):
     n, c = normed_ref.shape
     copies = start_copies(w_ref, w_vmem, sems, 4, 18 * c)
     size = size_ref[0]
@@ -625,6 +653,10 @@
     gw_ref[2 * c : 3 * c, :] = dot(nt_ref[...], gv_ref[...]).astype(gw_ref.dtype)
     gw_ref[3 * c : 4 * c, :] = dot_tn(mixed_ref[...], top_ref[...]).astype(gw_ref.dtype)
 
+    halves = (None, (mine_ref, theirs_ref))
+    block = mine_ref.shape[1]
+    waits = [send_rows(gw_ref, 0, 18 * c, 4 * c, size_ref, halves, gw_sem, block)]
+
     for m in range(n // MB):
         at = slice(m * MB, (m + 1) * MB)
         grad_ref[at, :] = dot_nt(gq_ref[at, :], wq) + dot_nt(gk_ref[at, :], wk) + dot_nt(gv_ref[at, :], wv)
@@ -663,41 +695,58 @@
         place = lax.broadcasted_iota(jnp.int32, (MB, c), 0) + m * MB
         good = ((place >> 5) < size) & ((place & 31) < size)
         out_ref[at, :] = jnp.where(good, out_rows, 0.0).astype(BF16)
+    for wait in waits:
+        wait.wait()
 
 
 def attention(size, normed, weights, vec, resid, cot, stat):
     n, c = normed.shape
+    half = shape((8, weights.shape[0] // 32, c), BF16)
     full, wide = pltpu.VMEM((n, c), BF16), pltpu.VMEM((n, n), BF16)
     return call(attention_body,
-        [(shape((n, c), BF16), "v"), (shape((4 * c, c), BF16), "v"), (shape((n, c), F32), "v"),
+        [(shape((n, c), BF16), "v"), (half, "a"), (half, "a"), (shape((n, c), F32), "v"),
          (shape((n + 64, 3 * c), BF16), "v"), (shape((8, c), F32), "v")],
         [(size, "s"), (normed, "v"), (weights, "a"), (vec, "v"), (resid, "v"), (cot, "v"), (stat, "v")],
-        [pltpu.VMEM((4 * c, c), BF16), full, full, full, wide, wide, full, full, full, full, full, full,
+        [pltpu.VMEM((4 * c, c), BF16), pltpu.SemaphoreType.DMA, pltpu.VMEM((4 * c, c), BF16), full, full, full, wide, wide, full, full, full, full, full, full,
          pltpu.VMEM((c, n), BF16), pltpu.SemaphoreType.DMA((4,))],
         flops=2 * n * c * (12 * c + 7 * n), name="attention")
 
 
-def grad_kernel_body(e3_ref, at_ref, gk_ref, stage, sems):
-    c, n = at_ref.shape
-    copies = []
+def grad_kernel_body(at_ref, e3_ref, act_ref, *refs, row, kept):
+    *outs, stage, sems = refs[kept:]
+    halves = (outs[0:2], outs[2:4])
+    c, n = act_ref.shape
+    block = outs[0].shape[1]
+    waits = []
     for dy in range(3):
         for dx in range(3):
             tap = 3 * dy + dx
             lo = (2 - dy) * SIDE
-            value = dot(at_ref[...], e3_ref[lo : lo + n, dx * c : (dx + 1) * c])
-            stage[tap * c : (tap + 1) * c, :] = value.astype(gk_ref.dtype)
-            copy = pltpu.make_async_copy(stage.at[pl.ds(tap * c, c)], gk_ref.at[pl.ds(tap * c, c)], sems.at[tap])
-            copy.start()
-            copies.append(copy)
-    for copy in copies:
-        copy.wait()
-
-
-def grad_kernel(e3, at, name):
-    c, n = at.shape
-    return call(grad_kernel_body, [(shape((9 * c, c), BF16), "a")], [(e3, "v"), (at, "v")],
+            value = dot(act_ref[...], e3_ref[lo : lo + n, dx * c : (dx + 1) * c])
+            stage[tap * c : (tap + 1) * c, :] = value.astype(BF16)
+            waits.append(send_rows(stage, tap * c, row + tap * c, c, at_ref, halves, sems.at[tap], block))
+    for wait in waits:
+        wait.wait()
+
+
+def grad_kernel_two(at, e3, act, mine_high, theirs_high):
+    c, n = act.shape
+    half = shape(mine_high.shape, BF16)
+    return call(functools.partial(grad_kernel_body, row=9 * c, kept=2),
+        [(half, "a"), (half, "a"), (half, "a"), (half, "a")],
+        [(at, "s"), (e3, "v"), (act, "v"), (mine_high, "a"), (theirs_high, "a")],
         [pltpu.VMEM((9 * c, c), BF16), pltpu.SemaphoreType.DMA((9,))],
-        flops=2 * n * 9 * c * c, name=name)[0]
+        flops=2 * n * 9 * c * c, name="grad_kernel_two", aliases={3: 2, 4: 3})
+
+
+def grad_kernel_one(at, e3, act, mine_low, theirs_low):
+    c, n = act.shape
+    half = shape(mine_low.shape, BF16)
+    return call(functools.partial(grad_kernel_body, row=0, kept=2),
+        [(half, "a"), (half, "a")],
+        [(at, "s"), (e3, "v"), (act, "v"), (mine_low, "a"), (theirs_low, "a")],
+        [pltpu.VMEM((9 * c, c), BF16), pltpu.SemaphoreType.DMA((9,))],
+        flops=2 * n * 9 * c * c, name="grad_kernel_one", aliases={3: 0, 4: 1})
 
 
 def conv_back(e3_ref, k_ref, copies, out_ref):
@@ -792,6 +841,64 @@
 
 
 ALL = ("img", "band")
+CORE = [(b, b ^ 1) for b in range(4)]
+ACROSS_Y = [(b, b ^ 2) for b in range(4)]
+ACROSS_X = [(i, i ^ 1) for i in range(8)]
+PLANES = {
+    2: (((3, 2), (2, 3)), ((1, 2), (0, 3)), ((0, 2), (1, 3))),
+    0: (((0, 1), (1, 0)), ((2, 1), (3, 0)), ((3, 1), (2, 0))),
+}
+
+
+def wide(*parts):
+    total = parts[0].astype(F32)
+    for part in parts[1:]:
+        total = total + part.astype(F32)
+    return total
+
+
+def reduce_half(mine, theirs, first):
+    block, c = mine.shape[1:]
+    cut = block // 2
+    dims = (2, 2, 2, block, c)
+    other = lax.ppermute(theirs, "band", CORE).reshape(dims)
+    mine = mine.reshape(dims)
+
+    def chip(*index):
+        return (mine[index], other[index])
+
+    head, tail = slice(0, cut), slice(cut, block)
+    every = slice(None)
+    send_a = wide(*chip(1, every, every, head)).astype(BF16)
+    send_b = wide(*chip(every, 1, every, tail)).astype(BF16)
+    got_a = lax.ppermute(send_a, "img", ACROSS_X)
+    got_b = lax.ppermute(send_b, "band", ACROSS_Y)
+    next_a = wide(*chip(0, 1, every, head), got_a[1]).astype(BF16)
+    next_b = wide(*chip(1, 0, every, tail), got_b[1]).astype(BF16)
+    last_a = lax.ppermute(next_a, "band", ACROSS_Y)
+    last_b = lax.ppermute(next_b, "img", ACROSS_X)
+    sum_a = wide(*chip(0, 0, every, head), got_a[0], last_a)
+    sum_b = wide(*chip(0, 0, every, tail), got_b[0], last_b)
+    plane = jnp.concatenate([sum_a, sum_b], axis=1)
+    low = plane.astype(BF16)
+    z = lax.axis_index("img") // 2
+    parts = [lax.dynamic_index_in_dim(plane, jnp.clip(z - first, 0, 1), 0, False)]
+    for moves in PLANES[first]:
+        table = [0] * 4
+        for source, target in moves:
+            table[source] = target - first
+        sent = lax.dynamic_index_in_dim(low, jnp.array(table, jnp.int32)[z], 0, False)
+        pairs = [(2 * a + x, 2 * b + x) for a, b in moves for x in range(2)]
+        parts.append(lax.ppermute(sent, "img", pairs))
+    return parts
+
+
+def sum_everywhere(v):
+    for axis, pairs in (("band", CORE), ("band", ACROSS_Y), ("img", ACROSS_X)):
+        v = v + lax.ppermute(v, axis, pairs)
+    for bit in (2, 4):
+        v = v + lax.ppermute(v, "img", [(i, i ^ bit) for i in range(8)])
+    return v
 
 
 def whole_image(
@@ -808,7 +915,8 @@
     batch, height, width, c = images.shape
     n = width * width
     mine = lax.axis_index("band")
-    size = lax.dynamic_slice_in_dim(sizes, mine, 1)
+    place = lax.axis_index("img")
+    at = jnp.stack([lax.dynamic_index_in_dim(sizes, mine, 0, False), place % 2, mine // 2, mine % 2])
 
     def to_image(field):
         parts = field.reshape(batch, height * width, c)
@@ -821,20 +929,23 @@
     weights = lax.all_gather(matrix_weight.astype(BF16).reshape(-1, c), ALL, axis=0, tiled=True)
     img = to_image(images)
     cot = to_image(cotangent)
-    a3_one, at_one, stat_one = act_one(size, img, vector_weight)
-    conv_out, a3_two, at_two, stat_two = conv_one(size, a3_one, weights, vector_weight)
-    resid, normed, stat_three = conv_two(size, a3_two, weights, vector_weight, img)
-    out, gw, grad_resid, e3_two, v3 = attention(size, normed, weights, vector_weight, resid, cot, stat_three)
-    gk2 = grad_kernel(e3_two, at_two, "grad_kernel_two")
-    e3_one, v2 = back_two(size, e3_two, weights, vector_weight, conv_out, stat_two)
-    gk1 = grad_kernel(e3_one, at_one, "grad_kernel_one")
-    grad_in, v1 = back_one(size, e3_one, weights, vector_weight, img, stat_one, grad_resid)
+    a3_one, at_one, stat_one = act_one(at, img, vector_weight)
+    conv_out, a3_two, at_two, stat_two = conv_one(at, a3_one, weights, vector_weight)
+    resid, normed, stat_three = conv_two(at, a3_two, weights, vector_weight, img)
+    out, mine_high, theirs_high, grad_resid, e3_two, v3 = attention(
+        at, normed, weights, vector_weight, resid, cot, stat_three
+    )
+    mine_low, theirs_low, mine_high, theirs_high = grad_kernel_two(at, e3_two, at_two, mine_high, theirs_high)
+    high = reduce_half(mine_high, theirs_high, 2)
+    e3_one, v2 = back_two(at, e3_two, weights, vector_weight, conv_out, stat_two)
+    mine_low, theirs_low = grad_kernel_one(at, e3_one, at_one, mine_low, theirs_low)
+    low = reduce_half(mine_low, theirs_low, 0)
+    grad_in, v1 = back_one(at, e3_one, weights, vector_weight, img, stat_one, grad_resid)
     block_out = to_bands(out)
     input_grad = to_bands(grad_in).astype(F32)
     vecs = jnp.stack([v1[0], v1[1], v2[0], v2[1], v2[2], v3[0], v3[1], v3[2], v3[3], v3[4], v3[5]])
-    vector_grads = lax.psum(vecs, ALL)
-    low_grads = lax.psum_scatter(jnp.concatenate([gk1, gk2, gw]), ALL, scatter_dimension=0, tiled=True)
-    matrix_grads = low_grads.astype(F32).reshape(-1)
+    vector_grads = sum_everywhere(vecs)
+    matrix_grads = jnp.where(place < 4, wide(*low), wide(*high)).reshape(-1)
     matrix_moments = MOMENTUM * matrix_momentum + matrix_grads
     matrix_masters = matrix_weight - LR_MATRIX * (matrix_grads + MOMENTUM * matrix_moments)
     matrix_means = AVERAGE * matrix_average + (1.0 - AVERAGE) * matrix_masters
@@ -856,10 +967,10 @@
 
 
 def solution(mesh):
-    whole = mesh.shape["band"]
+    fits = mesh.shape["img"] == 8 and mesh.shape["band"] == 4
 
     def per_device(images, *rest):
-        step = whole_image if images.shape[0] == whole and SIDE == images.shape[2] else banded
+        step = whole_image if fits and images.shape[:3] == (4, 8, SIDE) else banded
         return step(images, *rest)
 
     return jax.shard_map(

time: 404 us -> 350 us (0.87)
  the two profiles are of different devices: /device:TPU:0 before, /device:TPU:28 now
where the time goes in v2:
time: 350 us; the launch traced here: 349 us
  waiting for transfers between devices  146 us (42%)
  Pallas kernels  100 us (29%)
  starting transfers between devices  47.4 us (14%)
  other arithmetic  22.3 us (6%)
  between operations  22.2 us (6%)
  local copies, waits for them, and re-layouts  10.3 us (3%)
    pallas_call x8, Pallas kernels, call(): pl.pallas_call(body, out_shape=[o for o, _ in outs], in_specs=[spaces[s]...  100 us
    all_gather x1, waiting for transfers between devices, whole_image(): lax.all_gather(matrix_weight.astype(BF16).reshape(-1, c), ALL, axis=0, ti...  65 us
    ppermute x6, waiting for transfers between devices, reduce_half(): parts.append(lax.ppermute(sent, 'img', pairs))  28.6 us
    ppermute x2, waiting for transfers between devices, reduce_half(): got_b = lax.ppermute(send_b, 'band', ACROSS_Y)  24 us
    ppermute x6, starting transfers between devices, reduce_half(): parts.append(lax.ppermute(sent, 'img', pairs))  14.2 us
    all_to_all x2, waiting for transfers between devices, to_image(): return lax.all_to_all(parts, 'band', 0, 0, tiled=True).reshape(n, c)  13.6 us
    all_to_all x2, starting transfers between devices, to_bands(): lax.all_to_all(parts, 'band', 0, 0, tiled=True)  11.2 us
    ppermute x2, waiting for transfers between devices, reduce_half(): last_b = lax.ppermute(next_b, 'img', ACROSS_X)  9.3 us
  transfers between devices with their start and end apart: 26, of which 9 were waited for; matrix products, arithmetic and copies ran while one was open for 7% of the time, Pallas kernels for 12%

profile of v2, /device:TPU:28, one launch (start us, length us, event | category | flops | bytes accessed | tf_op | source)
XLA Modules:
  0.0 348.8 jit_solution(18420174610343634993)
XLA Ops:
  7.2 1.1 convert_element_type.225
  8.4 1.0 reshape.120
  9.4 4.0 %all-to-all-start = ((bf16[4,256,512]{2,1,0:T(8,128)(2,1)}), bf16[4,256,512]{2,1,0:T(8,128)(2,1)S(1)}, u32[]{:S(2)}, u32[]{:S(2)}) async-start(bf16[4,256,512]{2,1,0:T(8,128)(2,1)} %bitcast.148), calls=%async_computation | async-start | bytes 2097152 | tf_op jit(solution)/shard_map/all_to_all | solution.py:923
  13.4 0.6 dynamic_slice.48
  14.0 1.2 pad_add_fusion.size_ref.at_ref
  15.2 13.5 %all-to-all-done = bf16[4,256,512]{2,1,0:T(8,128)(2,1)S(1)} async-done(((bf16[4,256,512]{2,1,0:T(8,128)(2,1)}), bf16[4,256,512]{2,1,0:T(8,128)(2,1)S(1)}, u32[]{:S(2)}, u32[]{:S(2)}) %all-to-all-start) | async-done | bytes 1048608 | tf_op jit(solution)/shard_map/all_to_all | solution.py:923
  28.7 5.2 %all-to-all-start.1 = ((bf16[4,256,512]{2,1,0:T(8,128)(2,1)}), bf16[4,256,512]{2,1,0:T(8,128)(2,1)S(1)}, u32[]{:S(2)}, u32[]{:S(2)}) async-start(bf16[4,256,512]{2,1,0:T(8,128)(2,1)} %bitcast.5), calls=%async_computation.1 | async-start | bytes 2097152 | tf_op jit(solution)/shard_map/all_to_all | solution.py:923
  33.9 5.4 %act_one.1 = (bf16[1088,1536]{1,0:T(8,128)(2,1)}, bf16[512,1024]{1,0:T(8,128)(2,1)}, f32[8,512]{1,0:T(8,128)}) custom-call(s32[4]{0:T(128)} %pad_add_fusion.size_ref.at_ref, bf16[1024,512]{1,0:T(8,128)(2,1)} %bitcast.122, f32[11,512]{1,0:T(8,128)} %vec_ref.11), custom_call_target="tpu_custom_call" | custom-call | bytes 5478416 | tf_op jit(solution)/shard_map/act_one/pallas_call | solution.py:338
  39.3 65.0 %all-gather.2.cloned.1.call-done.k_ref.w_ref = bf16[11264,512]{1,0:T(8,128)(2,1)} async-done(((bf16[352,512]{1,0:T(8,128)(2,1)}), bf16[11264,512]{1,0:T(8,128)(2,1)}) %all-gather.2.cloned.1.call-update) | async-done | bytes 11534352 | tf_op jit(solution)/shard_map/all_gather | solution.py:929
  104.3 13.2 %conv_one.1 = (f32[1024,512]{1,0:T(8,128)}, bf16[1088,1536]{1,0:T(8,128)(2,1)}, bf16[512,1024]{1,0:T(8,128)(2,1)}, f32[8,512]{1,0:T(8,128)}) custom-call(s32[4]{0:T(128)} %pad_add_fusion.size_ref.at_ref, bf16[1088,1536]{1,0:T(8,128)(2,1)} %get-tuple-element.36.a3_ref, bf16[11264,512]{1,0:T(8,128)(2,1)} %all-gather.2.cloned.1.call-done.k_ref.w_ref, ...), custom_call_target="tpu_custom_call" | custom-call | flops 4831838208 | bytes 21403664 | tf_op jit(solution)/shard_map/conv_one/pallas_call | solution.py:338
  117.5 11.6 %conv_two.1 = (f32[1024,512]{1,0:T(8,128)}, bf16[1024,512]{1,0:T(8,128)(2,1)}, f32[8,512]{1,0:T(8,128)}) custom-call(s32[4]{0:T(128)} %pad_add_fusion.size_ref.at_ref, bf16[1088,1536]{1,0:T(8,128)(2,1)} %get-tuple-element.37.a3_ref, bf16[11264,512]{1,0:T(8,128)(2,1)} %all-gather.2.cloned.1.call-done.k_ref.w_ref, f32[11,512]{1,0:T(8,128)} %vec_ref.11, ...), custom_call_target="tpu_custom_call" | custom-call | flops 4831838208 | bytes 19109904 | tf_op jit(solution)/shard_map/conv_two/pallas_call | solution.py:338
  129.1 1.0 copy-done.7
  130.1 26.6 %attention.1 = (bf16[1024,512]{1,0:T(8,128)(2,1)}, bf16[8,352,512]{2,1,0:T(8,128)(2,1)}, bf16[8,352,512]{2,1,0:T(8,128)(2,1)}, f32[1024,512]{1,0:T(8,128)}, bf16...) custom-call(s32[4]{0:T(128)} %pad_add_fusion.size_ref.at_ref, bf16[1024,512]{1,0:T(8,128)(2,1)} %get-tuple-element.38.normed_ref, ...), custom_call_target="tpu_custom_call" | custom-call | flops 13958643712 | bytes 28039184 | tf_op jit(solution)/shard_map/attention/pallas_call | solution.py:338
  156.7 8.2 %grad_kernel_two.1 = (bf16[8,352,512]{2,1,0:T(8,128)(2,1)}, bf16[8,352,512]{2,1,0:T(8,128)(2,1)}, bf16[8,352,512]{2,1,0:T(8,128)(2,1)}, bf16[8,352,512]{2,1,0:T(8,128)(2,1)}) custom-call(s32[4]{0:T(128)} %pad_add_fusion.size_ref.at_ref, bf16[1088,1536]{1,0:T(8,128)(2,1)} %get-tuple-element.42.e3_ref, ...), custom_call_target="tpu_custom_call", output_to_operand_aliasing={{2}: (3, {}), {3}: (4, {})} | custom-call | flops 4831838208 | bytes 21692432 | tf_op jit(solution)/shard_map/grad_kernel_two/pallas_call | solution.py:338
  164.9 13.9 %back_two.1 = (bf16[1088,1536]{1,0:T(8,128)(2,1)}, f32[8,512]{1,0:T(8,128)}) custom-call(s32[4]{0:T(128)} %pad_add_fusion.size_ref.at_ref, bf16[1088,1536]{1,0:T(8,128)(2,1)} %get-tuple-element.42.e3_ref, bf16[11264,512]{1,0:T(8,128)(2,1)} %all-gather.2.cloned.1.call-done.k_ref.w_ref, f32[11,512]{1,0:T(8,128)} %vec_ref.11, ...), custom_call_target="tpu_custom_call" | custom-call | flops 4831838208 | bytes 20371472 | tf_op jit(solution)/shard_map/back_two/pallas_call | solution.py:338
  178.8 8.2 %grad_kernel_one.1 = (bf16[8,352,512]{2,1,0:T(8,128)(2,1)}, bf16[8,352,512]{2,1,0:T(8,128)(2,1)}) custom-call(s32[4]{0:T(128)} %pad_add_fusion.size_ref.at_ref, bf16[1088,1536]{1,0:T(8,128)(2,1)} %get-tuple-element.45.e3_ref, bf16[512,1024]{1,0:T(8,128)(2,1)} %get-tuple-element.49.act_ref, ...), custom_call_target="tpu_custom_call", output_to_operand_aliasing={{0}: (3, {}), {1}: (4, {})} | custom-call | flops 4831838208 | bytes 15925264 | tf_op jit(solution)/shard_map/grad_kernel_one/pallas_call | solution.py:338
  187.0 0.3 collective-permute-start
  187.6 13.2 %back_one.1 = (bf16[1024,512]{1,0:T(8,128)(2,1)}, f32[8,512]{1,0:T(8,128)}) custom-call(s32[4]{0:T(128)} %pad_add_fusion.size_ref.at_ref, bf16[1088,1536]{1,0:T(8,128)(2,1)} %get-tuple-element.45.e3_ref, bf16[11264,512]{1,0:T(8,128)(2,1)} %all-gather.2.cloned.1.call-done.k_ref.w_ref, f32[11,512]{1,0:T(8,128)} %vec_ref.11, bf16[1024,512]{1,0:T(8,128)(2,1)} %bitcast.124, ...), custom_call_target="tpu_custom_call" | custom-call | flops 4831838208 | bytes 19126288 | tf_op jit(solution)/shard_map/back_one/pallas_call | solution.py:338
  200.8 0.9 slice.148
  202.0 1.8 fusion.3
  203.8 0.7 collective-permute-start.3
  204.5 1.3 fusion.2
  205.8 1.4 collective-permute-start.1
  207.5 0.6 collective-permute-start.11
  208.1 1.1 fusion.4
  209.2 1.5 collective-permute-start.9
  210.7 12.2 %collective-permute-done.3 = bf16[2,2,176,512]{3,2,1,0:T(8,128)(2,1)S(1)} collective-permute-done((bf16[2,2,176,512]{3,2,1,0:T(8,128)(2,1)S(1)}, bf16[2,2,176,512]{3,2,1,0:T(8,128)(2,1)S(1)}, u32[]{:S(2)}, u32[]{:S(2)}) %collective-permute-start.3) | collective-permute-done | bytes 720928 | tf_op jit(solution)/shard_map/ppermute | solution.py:875
  222.9 1.1 fusion.22
  224.1 0.6 collective-permute-start.4
  224.7 1.5 collective-permute-start.17
  226.2 11.8 %collective-permute-done.11 = bf16[2,2,176,512]{3,2,1,0:T(8,128)(2,1)S(1)} collective-permute-done((bf16[2,2,176,512]{3,2,1,0:T(8,128)(2,1)S(1)}, bf16[2,2,176,512]{3,2,1,0:T(8,128)(2,1)S(1)}, u32[]{:S(2)}, u32[]{:S(2)}) %collective-permute-start.11) | collective-permute-done | bytes 720928 | tf_op jit(solution)/shard_map/ppermute | solution.py:875
  238.1 0.6 collective-permute-start.12
  238.8 9.3 %collective-permute-done.4 = bf16[2,176,512]{2,1,0:T(8,128)(2,1)S(1)} collective-permute-done((bf16[2,176,512]{2,1,0:T(8,128)(2,1)S(1)}, bf16[2,176,512]{2,1,0:T(8,128)(2,1)S(1)}, u32[]{:S(2)}, u32[]{:S(2)}) %collective-permute-start.4) | collective-permute-done | bytes 360480 | tf_op jit(solution)/shard_map/ppermute | solution.py:879
  248.1 1.6 fusion.23
  249.7 1.5 collective-permute-start.2
  251.2 0.6 collective-permute-start.18
  251.8 3.6 %collective-permute-done.18 = f32[11,512]{1,0:T(8,128)S(1)} collective-permute-done((f32[11,512]{1,0:T(8,128)S(1)}, f32[11,512]{1,0:T(8,128)S(1)}, u32[]{:S(2)}, u32[]{:S(2)}) %collective-permute-start.18) | collective-permute-done | bytes 22560 | tf_op jit(solution)/shard_map/ppermute | solution.py:898
  255.4 1.5 collective-permute-start.19
  256.9 0.6 dynamic_slice.50
  258.8 0.6 dynamic_slice.52
  260.7 0.6 dynamic_slice.54
  262.6 0.6 dynamic_slice.61
  267.1 5.0 %all-to-all-start.3 = ((bf16[4,256,512]{2,1,0:T(8,128)(2,1)}), bf16[4,256,512]{2,1,0:T(8,128)(2,1)S(1)}, u32[]{:S(2)}, u32[]{:S(2)}) async-start(bf16[4,256,512]{2,1,0:T(8,128)(2,1)} %bitcast.9), calls=%async_computation.3 | async-start | bytes 2097152 | tf_op jit(solution)/shard_map/all_to_all | solution.py:927
  272.1 1.3 collective-permute-start.20
  273.4 2.6 fusion.19
  276.1 1.4 fusion.25
  277.5 1.0 dynamic-slice_bitcast_fusion.5
  278.6 1.4 collective-permute-start.5
  280.0 6.3 %collective-permute-start.6 = (bf16[352,512]{1,0:T(8,128)(2,1)}, bf16[352,512]{1,0:T(8,128)(2,1)}, u32[]{:S(2)}, u32[]{:S(2)}) collective-permute-start(bf16[352,512]{1,0:T(8,128)(2,1)} %get-tuple-element.75), channel_id=1, source_target_pairs={{16,8},{20,12},{24,0},{28,4},{17,9},{21,13},{25,1},{29,5},{18,10},... | collective-permute-start | bytes 1081352 | tf_op jit(solution)/shard_map/ppermute | solution.py:892
  286.3 2.0 collective-permute-start.7
  288.3 6.2 %all-to-all-start.2 = ((bf16[4,256,512]{2,1,0:T(8,128)(2,1)}), bf16[4,256,512]{2,1,0:T(8,128)(2,1)}, u32[]{:S(2)}, u32[]{:S(2)}) async-start(bf16[4,256,512]{2,1,0:T(8,128)(2,1)} %bitcast.149), calls=%async_computation.2 | async-start | bytes 2097152 | tf_op jit(solution)/shard_map/all_to_all | solution.py:927
  294.5 1.5 fusion.21
  296.1 0.9 dynamic-slice_bitcast_fusion.2
  297.0 1.9 collective-permute-start.13
  299.0 1.3 collective-permute-start.14
  300.3 1.3 collective-permute-start.15
  301.6 0.7 multiply_add_fusion.2
  302.3 2.8 convert.9
  305.1 2.3 all-to-all-done.2
  307.4 10.0 %collective-permute-done.13 = bf16[352,512]{1,0:T(8,128)(2,1)} collective-permute-done((bf16[352,512]{1,0:T(8,128)(2,1)}, bf16[352,512]{1,0:T(8,128)(2,1)}, u32[]{:S(2)}, u32[]{:S(2)}) %collective-permute-start.13) | collective-permute-done | bytes 360480 | tf_op jit(solution)/shard_map/ppermute | solution.py:892
  317.4 18.6 %collective-permute-done.15 = bf16[352,512]{1,0:T(8,128)(2,1)} collective-permute-done((bf16[352,512]{1,0:T(8,128)(2,1)S(1)}, bf16[352,512]{1,0:T(8,128)(2,1)}, u32[]{:S(2)}, u32[]{:S(2)}) %collective-permute-start.15) | collective-permute-done | bytes 360480 | tf_op jit(solution)/shard_map/ppermute | solution.py:892
  336.0 1.9 fusion.12
  338.1 1.5 multiply_add_fusion
  339.7 2.3 copy.35
  (78 shorter events, 1.6 us)
Async XLA Ops:
  7.2 6.2 %copy-start.18 = (s32[4]{0:T(128)S(1)}, s32[4]{0:T(128)}, u32[]{:S(2)}) copy-start(s32[4]{0:T(128)} %param.17) | copy-start | bytes 52
  7.2 97.1 %all-gather.2.cloned.1.call-start = ((), (), s32[]{:S(2)}) async-start(), calls=%async_computation.4 | async-start | bytes 11894784 | tf_op jit(solution)/shard_map/all_gather | solution.py:929
  9.4 19.4 %all-to-all-start = ((bf16[4,256,512]{2,1,0:T(8,128)(2,1)}), bf16[4,256,512]{2,1,0:T(8,128)(2,1)S(1)}, u32[]{:S(2)}, u32[]{:S(2)}) async-start(bf16[4,256,512]{2,1,0:T(8,128)(2,1)} %bitcast.148), calls=%async_computation | async-start | bytes 2097152 | tf_op jit(solution)/shard_map/all_to_all | solution.py:923
  28.7 5.2 %copy-start = (bf16[4,256,512]{2,1,0:T(8,128)(2,1)}, bf16[4,256,512]{2,1,0:T(8,128)(2,1)S(1)}, u32[]{:S(2)}) copy-start(bf16[4,256,512]{2,1,0:T(8,128)(2,1)S(1)} %all-to-all-done) | copy-start | bytes 3145732
  28.7 100.3 %all-to-all-start.1 = ((bf16[4,256,512]{2,1,0:T(8,128)(2,1)}), bf16[4,256,512]{2,1,0:T(8,128)(2,1)S(1)}, u32[]{:S(2)}, u32[]{:S(2)}) async-start(bf16[4,256,512]{2,1,0:T(8,128)(2,1)} %bitcast.5), calls=%async_computation.1 | async-start | bytes 2097152 | tf_op jit(solution)/shard_map/all_to_all | solution.py:923
  129.1 1.1 copy-start.7
  187.0 15.0 %collective-permute-start = (bf16[8,352,512]{2,1,0:T(8,128)(2,1)}, bf16[8,352,512]{2,1,0:T(8,128)(2,1)S(1)}, u32[]{:S(2)}, u32[]{:S(2)}) collective-permute-start(bf16[8,352,512]{2,1,0:T(8,128)(2,1)} %get-tuple-element.56), channel_id=1, source_target_pairs={{0,1},{1,0},{2,3},{3,2},{4,5},{5,4},{6,7},{7,6},{8,9},{9,8},{10,11... | collective-permute-start | bytes 8650760 | tf_op jit(solution)/shard_map/ppermute | solution.py:864
  187.3 19.9 %collective-permute-start.8 = (bf16[8,352,512]{2,1,0:T(8,128)(2,1)}, bf16[8,352,512]{2,1,0:T(8,128)(2,1)S(1)}, u32[]{:S(2)}, u32[]{:S(2)}) collective-permute-start(bf16[8,352,512]{2,1,0:T(8,128)(2,1)} %get-tuple-element.58), channel_id=1, source_target_pairs={{0,1},{1,0},{2,3},{3,2},{4,5},{5,4},{6,7},{7,6},{8,9},{9,8},{10,11... | collective-permute-start | bytes 8650760 | tf_op jit(solution)/shard_map/ppermute | solution.py:864
  187.6 14.1 %copy-start.17 = (f32[8,512]{1,0:T(8,128)S(1)}, f32[8,512]{1,0:T(8,128)}, u32[]{:S(2)}) copy-start(f32[8,512]{1,0:T(8,128)} %get-tuple-element.60) | copy-start | bytes 49156
  187.6 14.1 %copy-start.14 = (f32[8,512]{1,0:T(8,128)S(1)}, f32[8,512]{1,0:T(8,128)}, u32[]{:S(2)}) copy-start(f32[8,512]{1,0:T(8,128)} %get-tuple-element.61) | copy-start | bytes 49156
  200.8 6.5 %copy-start.6 = (bf16[8,352,512]{2,1,0:T(8,128)(2,1)S(1)}, bf16[8,352,512]{2,1,0:T(8,128)(2,1)}, u32[]{:S(2)}) copy-start(bf16[8,352,512]{2,1,0:T(8,128)(2,1)} %get-tuple-element.57) | copy-start | bytes 8650756
  201.7 22.9 %collective-permute-start.16 = (f32[11,512]{1,0:T(8,128)S(1)}, f32[11,512]{1,0:T(8,128)S(1)}, u32[]{:S(2)}, u32[]{:S(2)}) collective-permute-start(f32[11,512]{1,0:T(8,128)S(1)} %pad_maximum_fusion.2), channel_id=1, source_target_pairs={{0,1},{1,0},{2,3},{3,2},{4,5},{5,4},{6,7},{7,6},{8,9},{9,8},{10,11... | collective-permute-start | bytes 67592 | tf_op jit(solution)/shard_map/ppermute | solution.py:898
  202.0 20.9 %copy-start.5 = (bf16[8,352,512]{2,1,0:T(8,128)(2,1)}, bf16[8,352,512]{2,1,0:T(8,128)(2,1)S(1)}, u32[]{:S(2)}) copy-start(bf16[8,352,512]{2,1,0:T(8,128)(2,1)S(1)} %collective-permute-done) | copy-start | bytes 8650756
  203.8 19.0 %collective-permute-start.3 = (bf16[2,2,176,512]{3,2,1,0:T(8,128)(2,1)S(1)}, bf16[2,2,176,512]{3,2,1,0:T(8,128)(2,1)S(1)}, u32[]{:S(2)}, u32[]{:S(2)}) collective-permute-start(bf16[2,2,176,512]{3,2,1,0:T(8,128)(2,1)S(1)} %fusion.3), channel_id=1, source_target_pairs={{0,2},{1,3},{2,0},{3,1},{4,6},{5,7},{6,4},{7,5},{8,10},{9,11},{10,... | collective-permute-start | bytes 2162696 | tf_op jit(solution)/shard_map/ppermute | solution.py:875
  205.8 33.0 %collective-permute-start.1 = (bf16[2,2,176,512]{3,2,1,0:T(8,128)(2,1)S(1)}, bf16[2,2,176,512]{3,2,1,0:T(8,128)(2,1)S(1)}, u32[]{:S(2)}, u32[]{:S(2)}) collective-permute-start(bf16[2,2,176,512]{3,2,1,0:T(8,128)(2,1)S(1)} %fusion.2), channel_id=1, source_target_pairs={{0,4},{4,0},{8,12},{12,8},{16,20},{20,16},{24,28},{28,24},{1,5},{5... | collective-permute-start | bytes 2162696 | tf_op jit(solution)/shard_map/ppermute | solution.py:874
  207.3 30.7 %copy-start.4 = (bf16[8,352,512]{2,1,0:T(8,128)(2,1)}, bf16[8,352,512]{2,1,0:T(8,128)(2,1)S(1)}, u32[]{:S(2)}) copy-start(bf16[8,352,512]{2,1,0:T(8,128)(2,1)S(1)} %collective-permute-done.8) | copy-start | bytes 8650756
  207.5 30.5 %collective-permute-start.11 = (bf16[2,2,176,512]{3,2,1,0:T(8,128)(2,1)S(1)}, bf16[2,2,176,512]{3,2,1,0:T(8,128)(2,1)S(1)}, u32[]{:S(2)}, u32[]{:S(2)}) collective-permute-start(bf16[2,2,176,512]{3,2,1,0:T(8,128)(2,1)S(1)} %fusion.5), channel_id=1, source_target_pairs={{0,2},{1,3},{2,0},{3,1},{4,6},{5,7},{6,4},{7,5},{8,10},{9,11},{10,... | collective-permute-start | bytes 2162696 | tf_op jit(solution)/shard_map/ppermute | solution.py:875
  209.2 64.2 %collective-permute-start.9 = (bf16[2,2,176,512]{3,2,1,0:T(8,128)(2,1)}, bf16[2,2,176,512]{3,2,1,0:T(8,128)(2,1)}, u32[]{:S(2)}, u32[]{:S(2)}) collective-permute-start(bf16[2,2,176,512]{3,2,1,0:T(8,128)(2,1)} %fusion.4), channel_id=1, source_target_pairs={{0,4},{4,0},{8,12},{12,8},{16,20},{20,16},{24,28},{28,24},{1,5},{5... | collective-permute-start | bytes 2162696 | tf_op jit(solution)/shard_map/ppermute | solution.py:874
  224.0 32.9 %copy-start.22 = (s32[4]{0:T(128)S(1)}, s32[4]{0:T(128)}, u32[]{:S(2)}) copy-start(s32[4]{0:T(128)} %constant.100.clone) | copy-start | bytes 52
  224.0 34.8 %copy-start.21 = (s32[4]{0:T(128)S(1)}, s32[4]{0:T(128)}, u32[]{:S(2)}) copy-start(s32[4]{0:T(128)} %constant.99.clone) | copy-start | bytes 52
  224.0 36.7 %copy-start.20 = (s32[4]{0:T(128)S(1)}, s32[4]{0:T(128)}, u32[]{:S(2)}) copy-start(s32[4]{0:T(128)} %constant.102.clone) | copy-start | bytes 52
  224.1 38.6 %copy-start.19 = (s32[4]{0:T(128)S(1)}, s32[4]{0:T(128)}, u32[]{:S(2)}) copy-start(s32[4]{0:T(128)} %constant.101.clone) | copy-start | bytes 52
  224.1 24.0 %collective-permute-start.4 = (bf16[2,176,512]{2,1,0:T(8,128)(2,1)S(1)}, bf16[2,176,512]{2,1,0:T(8,128)(2,1)S(1)}, u32[]{:S(2)}, u32[]{:S(2)}) collective-permute-start(bf16[2,176,512]{2,1,0:T(8,128)(2,1)S(1)} %fusion.22), channel_id=1, source_target_pairs={{0,4},{4,0},{8,12},{12,8},{16,20},{20,16},{24,28},{28,24},{1,5},{5... | collective-permute-start | bytes 1081352 | tf_op jit(solution)/shard_map/ppermute | solution.py:879
  224.7 26.5 %collective-permute-start.17 = (f32[11,512]{1,0:T(8,128)S(1)}, f32[11,512]{1,0:T(8,128)S(1)}, u32[]{:S(2)}, u32[]{:S(2)}) collective-permute-start(f32[11,512]{1,0:T(8,128)S(1)} %fusion.26), channel_id=1, source_target_pairs={{0,2},{1,3},{2,0},{3,1},{4,6},{5,7},{6,4},{7,5},{8,10},{9,11},{10,... | collective-permute-start | bytes 67592 | tf_op jit(solution)/shard_map/ppermute | solution.py:898
  238.0 11.7 %copy-start.12 = (bf16[2,2,176,512]{3,2,1,0:T(8,128)(2,1)}, bf16[2,2,176,512]{3,2,1,0:T(8,128)(2,1)S(1)}, u32[]{:S(2)}) copy-start(bf16[2,2,176,512]{3,2,1,0:T(8,128)(2,1)S(1)} %collective-permute-done.11) | copy-start | bytes 2162692
  238.1 35.3 %collective-permute-start.12 = (bf16[2,176,512]{2,1,0:T(8,128)(2,1)S(1)}, bf16[2,176,512]{2,1,0:T(8,128)(2,1)S(1)}, u32[]{:S(2)}, u32[]{:S(2)}) collective-permute-start(bf16[2,176,512]{2,1,0:T(8,128)(2,1)S(1)} %fusion.18), channel_id=1, source_target_pairs={{0,4},{4,0},{8,12},{12,8},{16,20},{20,16},{24,28},{28,24},{1,5},{5... | collective-permute-start | bytes 1081352 | tf_op jit(solution)/shard_map/ppermute | solution.py:879
  238.8 9.3 %copy-start.10 = (bf16[2,2,176,512]{3,2,1,0:T(8,128)(2,1)}, bf16[2,2,176,512]{3,2,1,0:T(8,128)(2,1)S(1)}, u32[]{:S(2)}) copy-start(bf16[2,2,176,512]{3,2,1,0:T(8,128)(2,1)S(1)} %collective-permute-done.1) | copy-start | bytes 2162692
  249.7 26.3 %collective-permute-start.2 = (bf16[2,176,512]{2,1,0:T(8,128)(2,1)S(1)}, bf16[2,176,512]{2,1,0:T(8,128)(2,1)}, u32[]{:S(2)}, u32[]{:S(2)}) collective-permute-start(bf16[2,176,512]{2,1,0:T(8,128)(2,1)S(1)} %get-tuple-element.70), channel_id=1, source_target_pairs={{0,2},{1,3},{2,0},{3,1},{4,6},{5,7},{6,4},{7,5},{8,10},{9,11},{10,... | collective-permute-start | bytes 1081352 | tf_op jit(solution)/shard_map/ppermute | solution.py:878
  251.2 4.2 %collective-permute-start.18 = (f32[11,512]{1,0:T(8,128)S(1)}, f32[11,512]{1,0:T(8,128)S(1)}, u32[]{:S(2)}, u32[]{:S(2)}) collective-permute-start(f32[11,512]{1,0:T(8,128)S(1)} %add.247), channel_id=1, source_target_pairs={{0,4},{4,0},{8,12},{12,8},{16,20},{20,16},{24,28},{28,24},{1,5},{5... | collective-permute-start | bytes 67592 | tf_op jit(solution)/shard_map/ppermute | solution.py:898
  255.4 16.6 %collective-permute-start.19 = (f32[11,512]{1,0:T(8,128)S(1)}, f32[11,512]{1,0:T(8,128)S(1)}, u32[]{:S(2)}, u32[]{:S(2)}) collective-permute-start(f32[11,512]{1,0:T(8,128)S(1)} %add.248), channel_id=1, source_target_pairs={{0,8},{4,12},{8,0},{12,4},{16,24},{20,28},{24,16},{28,20},{1,9},{5... | collective-permute-start | bytes 67592 | tf_op jit(solution)/shard_map/ppermute | solution.py:900
  267.1 21.2 %all-to-all-start.3 = ((bf16[4,256,512]{2,1,0:T(8,128)(2,1)}), bf16[4,256,512]{2,1,0:T(8,128)(2,1)S(1)}, u32[]{:S(2)}, u32[]{:S(2)}) async-start(bf16[4,256,512]{2,1,0:T(8,128)(2,1)} %bitcast.9), calls=%async_computation.3 | async-start | bytes 2097152 | tf_op jit(solution)/shard_map/all_to_all | solution.py:927
  272.1 4.0 %copy-start.11 = (bf16[2,2,176,512]{3,2,1,0:T(8,128)(2,1)S(1)}, bf16[2,2,176,512]{3,2,1,0:T(8,128)(2,1)}, u32[]{:S(2)}) copy-start(bf16[2,2,176,512]{3,2,1,0:T(8,128)(2,1)} %copy-done.10) | copy-start | bytes 2162692
  272.1 26.9 %collective-permute-start.20 = (f32[11,512]{1,0:T(8,128)S(1)}, f32[11,512]{1,0:T(8,128)S(1)}, u32[]{:S(2)}, u32[]{:S(2)}) collective-permute-start(f32[11,512]{1,0:T(8,128)S(1)} %add.249), channel_id=1, source_target_pairs={{0,16},{4,20},{8,24},{12,28},{16,0},{20,4},{24,8},{28,12},{1,17},{... | collective-permute-start | bytes 67592 | tf_op jit(solution)/shard_map/ppermute | solution.py:900
  276.0 18.5 %collective-permute-start.10 = (bf16[2,176,512]{2,1,0:T(8,128)(2,1)}, bf16[2,176,512]{2,1,0:T(8,128)(2,1)}, u32[]{:S(2)}, u32[]{:S(2)}) collective-permute-start(bf16[2,176,512]{2,1,0:T(8,128)(2,1)} %get-tuple-element.72), channel_id=1, source_target_pairs={{0,2},{1,3},{2,0},{3,1},{4,6},{5,7},{6,4},{7,5},{8,10},{9,11},{10,... | collective-permute-start | bytes 1081352 | tf_op jit(solution)/shard_map/ppermute | solution.py:878
  278.6 21.7 %collective-permute-start.5 = (bf16[352,512]{1,0:T(8,128)(2,1)}, bf16[352,512]{1,0:T(8,128)(2,1)}, u32[]{:S(2)}, u32[]{:S(2)}) collective-permute-start(bf16[352,512]{1,0:T(8,128)(2,1)} %get-tuple-element.73), channel_id=1, source_target_pairs={{0,8},{4,12},{8,0},{12,4},{1,9},{5,13},{9,1},{13,5},{2,10},{6,14},... | collective-permute-start | bytes 1081352 | tf_op jit(solution)/shard_map/ppermute | solution.py:892
  280.0 27.4 %collective-permute-start.6 = (bf16[352,512]{1,0:T(8,128)(2,1)}, bf16[352,512]{1,0:T(8,128)(2,1)}, u32[]{:S(2)}, u32[]{:S(2)}) collective-permute-start(bf16[352,512]{1,0:T(8,128)(2,1)} %get-tuple-element.75), channel_id=1, source_target_pairs={{16,8},{20,12},{24,0},{28,4},{17,9},{21,13},{25,1},{29,5},{18,10},... | collective-permute-start | bytes 1081352 | tf_op jit(solution)/shard_map/ppermute | solution.py:892
  286.3 21.1 %collective-permute-start.7 = (bf16[352,512]{1,0:T(8,128)(2,1)}, bf16[352,512]{1,0:T(8,128)(2,1)}, u32[]{:S(2)}, u32[]{:S(2)}) collective-permute-start(bf16[352,512]{1,0:T(8,128)(2,1)} %get-tuple-element.74), channel_id=1, source_target_pairs={{24,8},{28,12},{16,0},{20,4},{25,9},{29,13},{17,1},{21,5},{26,10},... | collective-permute-start | bytes 1081352 | tf_op jit(solution)/shard_map/ppermute | solution.py:892
  288.3 6.2 %copy-start.1 = (bf16[4,256,512]{2,1,0:T(8,128)(2,1)}, bf16[4,256,512]{2,1,0:T(8,128)(2,1)S(1)}, u32[]{:S(2)}) copy-start(bf16[4,256,512]{2,1,0:T(8,128)(2,1)S(1)} %all-to-all-done.3) | copy-start | bytes 3145732
  288.3 19.1 %all-to-all-start.2 = ((bf16[4,256,512]{2,1,0:T(8,128)(2,1)}), bf16[4,256,512]{2,1,0:T(8,128)(2,1)}, u32[]{:S(2)}, u32[]{:S(2)}) async-start(bf16[4,256,512]{2,1,0:T(8,128)(2,1)} %bitcast.149), calls=%async_computation.2 | async-start | bytes 2097152 | tf_op jit(solution)/shard_map/all_to_all | solution.py:927
  294.5 7.1 %copy-start.13 = (f32[11,512]{1,0:T(8,128)S(1)}, f32[11,512]{1,0:T(8,128)}, u32[]{:S(2)}) copy-start(f32[11,512]{1,0:T(8,128)} %vec_ref.11) | copy-start | bytes 67588
  294.5 7.1 %copy-start.15 = (f32[11,512]{1,0:T(8,128)S(1)}, f32[11,512]{1,0:T(8,128)}, u32[]{:S(2)}) copy-start(f32[11,512]{1,0:T(8,128)} %param.23) | copy-start | bytes 67588
  294.5 7.2 %copy-start.16 = (f32[11,512]{1,0:T(8,128)S(1)}, f32[11,512]{1,0:T(8,128)}, u32[]{:S(2)}) copy-start(f32[11,512]{1,0:T(8,128)} %param.22) | copy-start | bytes 67588
  297.0 20.4 %collective-permute-start.13 = (bf16[352,512]{1,0:T(8,128)(2,1)}, bf16[352,512]{1,0:T(8,128)(2,1)}, u32[]{:S(2)}, u32[]{:S(2)}) collective-permute-start(bf16[352,512]{1,0:T(8,128)(2,1)} %get-tuple-element.76), channel_id=1, source_target_pairs={{24,16},{28,20},{16,24},{20,28},{25,17},{29,21},{17,25},{21,29},{2... | collective-permute-start | bytes 1081352 | tf_op jit(solution)/shard_map/ppermute | solution.py:892
  299.0 18.5 %collective-permute-start.14 = (bf16[352,512]{1,0:T(8,128)(2,1)}, bf16[352,512]{1,0:T(8,128)(2,1)}, u32[]{:S(2)}, u32[]{:S(2)}) collective-permute-start(bf16[352,512]{1,0:T(8,128)(2,1)} %get-tuple-element.78), channel_id=1, source_target_pairs={{8,16},{12,20},{0,24},{4,28},{9,17},{13,21},{1,25},{5,29},{10,18},... | collective-permute-start | bytes 1081352 | tf_op jit(solution)/shard_map/ppermute | solution.py:892
  300.3 35.7 %collective-permute-start.15 = (bf16[352,512]{1,0:T(8,128)(2,1)S(1)}, bf16[352,512]{1,0:T(8,128)(2,1)}, u32[]{:S(2)}, u32[]{:S(2)}) collective-permute-start(bf16[352,512]{1,0:T(8,128)(2,1)S(1)} %get-tuple-element.77), channel_id=1, source_target_pairs={{0,16},{4,20},{8,24},{12,28},{1,17},{5,21},{9,25},{13,29},{2,18},{... | collective-permute-start | bytes 1081352 | tf_op jit(solution)/shard_map/ppermute | solution.py:892
  307.4 30.7 %copy-start.2 = (f32[180224]{0:T(1024)S(1)}, f32[180224]{0:T(1024)}, u32[]{:S(2)}) copy-start(f32[180224]{0:T(1024)} %param.18) | copy-start | bytes 2162692
  307.4 30.8 %copy-start.8 = (f32[180224]{0:T(1024)S(1)}, f32[180224]{0:T(1024)}, u32[]{:S(2)}) copy-start(f32[180224]{0:T(1024)} %param.20) | copy-start | bytes 2162692
  307.4 30.8 %copy-start.9 = (f32[180224]{0:T(1024)S(1)}, f32[180224]{0:T(1024)}, u32[]{:S(2)}) copy-start(f32[180224]{0:T(1024)} %param.19) | copy-start | bytes 2162692
  338.1 3.9 %copy-start.3 = (f32[44,4,8,128]{3,1,2,0:T(4,128)}, f32[44,4,8,128]{3,1,2,0:T(4,128)S(1)}, u32[]{:S(2)}) copy-start(f32[44,4,8,128]{3,1,2,0:T(4,128)S(1)} %copy.29) | copy-start | bytes 2162692
Sparse Core Ops, SparseCore 0:
  11.4 92.8 all-gather.1
